TPU v7x, 512 devices: a whole 4x8x8 slice. The times are simulated.
512 devices in a mesh: chan: 16 (over x, y_hi, core), tm: 32 (over z, y_lo).
Axes of the slice: x: 4, y: 8 (y_hi: 2, y_lo: 4; y = y_hi * 4 + y_lo), z: 8, core: 2. Of those that a mesh axis runs over, the one named last changes fastest.
Arguments:
- traces: bfloat16 [16, 128, 128, 512], P('chan', 'tm'), may hold values from -6 to 6
- pair_listed: int32 [16, 8], P('chan'), may hold values from 0 to 1, as said below
- owner_slot: int32 [16, 8], P('chan'), may hold values from 0 to 31, as said below
- window_count: int32 [16, 8, 32], P('chan'), may hold values from 1 to 4, as said below
Outputs:
- stacks: float32 [16, 32, 128, 128], P('chan', 'tm')
Inputs may be any that keep to these rules, and one draw needn't show every extreme that they name: `pair_listed`: every distance is listed for block 0. `owner_slot`: distinct within each block's row. `window_count`: the windows entering are the first ones of the group; 4 is reached in every draw.
All inputs are finite; a program needn't handle non-finite values.
Results may differ from a plain program's by a relative error of at most 0.015.
Values may be sent and summed in bfloat16 or wider, within the bound.
No kernel may reach another device: no remote copies, remote signals or barrier semaphores. Data moves between devices by JAX's collectives and lax.ppermute only.
A program may use at most 64 MiB of HBM per device.

v0:
```python
import math

import jax
import jax.numpy as jnp
from jax import lax
from jax.sharding import PartitionSpec as P

BAND = 64
SMOOTH = 16
OFFSETS = 128
LAGS = 128


WATER = 0.1
PRECISE = lax.Precision.HIGHEST


def passed_along(block, axis, distance):
    devices = range(lax.axis_size(axis))
    route = [((i - distance) % len(devices), i) for i in devices]
    return lax.ppermute(block, axis, route)


def angles(left_index, right_index, period):
    product = left_index[:, None] * right_index[None, :] % period
    return 2.0 * math.pi / period * product.astype(jnp.float32)


def smooth_matrix():
    source = jnp.arange(BAND, dtype=jnp.int32)[:, None]
    target = jnp.arange(BAND, dtype=jnp.int32)[None, :]
    start = jnp.clip(target - SMOOTH // 2, 0, BAND - SMOOTH)
    inside = (source >= start) & (source < start + SMOOTH)
    return inside.astype(jnp.float32) / SMOOTH


def split_table(table):
    table_high = table.astype(jnp.bfloat16)
    table_low = (table - table_high.astype(jnp.float32)).astype(jnp.bfloat16)
    return (table_high, table_low)


def whiten(traces_local):
    windows, channels, samples = traces_local.shape
    flat_rows = traces_local.reshape(windows * channels, samples)
    phase_turn = angles(
        jnp.arange(samples, dtype=jnp.int32), jnp.arange(BAND, dtype=jnp.int32) + 1, samples
    )
    band_table = jnp.concatenate([jnp.cos(phase_turn), -jnp.sin(phase_turn)], axis=1)
    table_high, table_low = split_table(band_table)
    spectrum = jnp.dot(flat_rows, table_high, preferred_element_type=jnp.float32)
    spectrum = spectrum + jnp.dot(flat_rows, table_low, preferred_element_type=jnp.float32)
    real_part = spectrum[:, :BAND]
    imag_part = spectrum[:, BAND:]
    amplitude = jnp.sqrt(real_part * real_part + imag_part * imag_part)
    local_mean = jnp.dot(amplitude, smooth_matrix(), precision=PRECISE)
    water_level = local_mean + WATER * jnp.mean(amplitude, axis=1, keepdims=True) + 1e-06
    whitened = spectrum / jnp.concatenate([water_level, water_level], axis=1)
    return whitened.astype(jnp.bfloat16).reshape(windows, channels, 2 * BAND)


def channel_spectrum(block_data):
    channels = block_data.shape[1]
    padded = 2 * channels
    phase_turn = angles(
        jnp.arange(channels, dtype=jnp.int32), jnp.arange(padded, dtype=jnp.int32), padded
    )
    cos_high, cos_low = split_table(jnp.cos(phase_turn))
    sin_high, sin_low = split_table(jnp.sin(phase_turn))
    with_cos = jnp.einsum("wcg,ck->wkg", block_data, cos_high, preferred_element_type=jnp.float32)
    with_cos = with_cos + jnp.einsum(
        "wcg,ck->wkg", block_data, cos_low, preferred_element_type=jnp.float32
    )
    with_sin = jnp.einsum("wcg,ck->wkg", block_data, sin_high, preferred_element_type=jnp.float32)
    with_sin = with_sin + jnp.einsum(
        "wcg,ck->wkg", block_data, sin_low, preferred_element_type=jnp.float32
    )
    spec_real = with_cos[..., :BAND] + with_sin[..., BAND:]
    spec_imag = with_cos[..., BAND:] - with_sin[..., :BAND]
    return (spec_real, spec_imag)


def pair_term(arrived, own_real, own_imag, window_used, weight):
    src_real, src_imag = channel_spectrum(arrived)
    windows = arrived.shape[0]
    window_keep = (jnp.arange(windows, dtype=jnp.int32) < window_used).astype(jnp.float32)[
        :, None, None
    ]
    cross_real = jnp.sum(window_keep * (src_real * own_real + src_imag * own_imag), axis=0)
    cross_imag = jnp.sum(window_keep * (src_real * own_imag - src_imag * own_real), axis=0)
    padded = cross_real.shape[0]
    offset_steps = jnp.arange(OFFSETS, dtype=jnp.int32) - OFFSETS // 2
    phase_turn = angles(offset_steps, jnp.arange(padded, dtype=jnp.int32), padded)
    back_cos = jnp.cos(phase_turn) / padded
    back_sin = jnp.sin(phase_turn) / padded
    part_real = jnp.dot(back_cos, cross_real, precision=PRECISE) - jnp.dot(
        back_sin, cross_imag, precision=PRECISE
    )
    part_imag = jnp.dot(back_sin, cross_real, precision=PRECISE) + jnp.dot(
        back_cos, cross_imag, precision=PRECISE
    )
    return weight * jnp.concatenate([part_real, part_imag], axis=1)


def shards(traces, pair_listed, owner_slot, window_count):
    samples = traces.shape[3]
    whitened = whiten(traces[0])
    own_real, own_imag = channel_spectrum(whitened)
    pair_span = pair_listed.shape[1]
    groups = window_count.shape[2]
    group_index = lax.axis_index("tm")
    picked = jnp.arange(groups, dtype=jnp.int32) == group_index
    counts_here = jnp.sum(jnp.where(picked[None, :], window_count[0], 0), axis=1)
    totals = jnp.sum(window_count[0], axis=1).astype(jnp.float32)
    weights = pair_listed[0].astype(jnp.float32) / totals
    pair_terms = []
    moving = whitened
    for shift_step in range(pair_span):
        moving = passed_along(moving, "chan", 1)
        pair_terms.append(
            pair_term(moving, own_real, own_imag, counts_here[shift_step], weights[shift_step])
        )
    partials = jnp.stack(pair_terms)
    owners = owner_slot[0]
    summed = lax.psum(partials, "tm")
    owned_mask = (owners == group_index).astype(jnp.float32)
    owned = jnp.sum(owned_mask[:, None, None] * summed, axis=0)
    lag_angle = angles(
        jnp.arange(BAND, dtype=jnp.int32) + 1,
        jnp.arange(LAGS, dtype=jnp.int32) - LAGS // 2,
        samples,
    )
    lag_cos = jnp.cos(lag_angle)
    lag_sin = jnp.sin(lag_angle)
    stacked = jnp.dot(owned[:, :BAND], lag_cos, precision=PRECISE) - jnp.dot(
        owned[:, BAND:], lag_sin, precision=PRECISE
    )
    stacked = stacked / math.sqrt(BAND)
    return stacked[None, None]


def solution(mesh):
    placed = (P("chan", "tm", None, None), P("chan", None), P("chan", None), P("chan", None, None))
    return jax.shard_map(
        shards, mesh=mesh, in_specs=placed, out_specs=P("chan", "tm", None, None), check_vma=False
    )
```

profile of v0, /device:TPU:2, one launch (start us, length us, event | category | flops | bytes accessed | tf_op | source)
XLA Modules:
  0.0 484.5 jit_solution(13503771856990752241)
XLA Ops:
  6.6 1.1 fusion.35
  9.0 1.9 collective-permute-start
  17.3 1.2 compare_convert_fusion.1
  18.5 1.3 compare_convert_fusion.3
  24.0 7.8 %collective-permute-start.1 = (bf16[4,128,128]{1,2,0:T(8,128)(2,1)S(1)}, bf16[4,128,128]{1,2,0:T(8,128)(2,1)S(1)}, u32[]{:S(2)}, u32[]{:S(2)}) collective-permute-start(bf16[4,128,128]{1,2,0:T(8,128)(2,1)S(1)} %collective-permute-done), channel_id=1, source_target_pairs={{480,0},{0,32},{32,64},{64,96},{96,128},{128,160},{160,192},{192,2... | collective-permute-start | bytes 393224 | tf_op jit(solution)/shard_map/ppermute | solution.py:21
  31.9 3.3 collective-permute-done.1
  38.1 2.1 collective-permute-start.2
  40.2 8.9 %collective-permute-done.2 = bf16[4,128,128]{1,2,0:T(8,128)(2,1)S(1)} collective-permute-done((bf16[4,128,128]{1,2,0:T(8,128)(2,1)S(1)}, bf16[4,128,128]{1,2,0:T(8,128)(2,1)S(1)}, u32[]{:S(2)}, u32[]{:S(2)}) %collective-permute-start.2) | collective-permute-done | bytes 131104 | tf_op jit(solution)/shard_map/ppermute | solution.py:21
  52.0 1.9 collective-permute-start.3
  54.0 10.6 %collective-permute-done.3 = bf16[4,128,128]{1,2,0:T(8,128)(2,1)S(1)} collective-permute-done((bf16[4,128,128]{1,2,0:T(8,128)(2,1)S(1)}, bf16[4,128,128]{1,2,0:T(8,128)(2,1)S(1)}, u32[]{:S(2)}, u32[]{:S(2)}) %collective-permute-start.3) | collective-permute-done | bytes 131104 | tf_op jit(solution)/shard_map/ppermute | solution.py:21
  67.5 1.9 collective-permute-start.4
  69.5 9.2 %collective-permute-done.4 = bf16[4,128,128]{1,2,0:T(8,128)(2,1)S(1)} collective-permute-done((bf16[4,128,128]{1,2,0:T(8,128)(2,1)S(1)}, bf16[4,128,128]{1,2,0:T(8,128)(2,1)S(1)}, u32[]{:S(2)}, u32[]{:S(2)}) %collective-permute-start.4) | collective-permute-done | bytes 131104 | tf_op jit(solution)/shard_map/ppermute | solution.py:21
  81.6 1.9 collective-permute-start.5
  83.6 9.1 %collective-permute-done.5 = bf16[4,128,128]{1,2,0:T(8,128)(2,1)S(1)} collective-permute-done((bf16[4,128,128]{1,2,0:T(8,128)(2,1)S(1)}, bf16[4,128,128]{1,2,0:T(8,128)(2,1)S(1)}, u32[]{:S(2)}, u32[]{:S(2)}) %collective-permute-start.5) | collective-permute-done | bytes 131104 | tf_op jit(solution)/shard_map/ppermute | solution.py:21
  95.5 1.9 collective-permute-start.6
  97.5 9.1 %collective-permute-done.6 = bf16[4,128,128]{1,2,0:T(8,128)(2,1)S(1)} collective-permute-done((bf16[4,128,128]{1,2,0:T(8,128)(2,1)S(1)}, bf16[4,128,128]{1,2,0:T(8,128)(2,1)S(1)}, u32[]{:S(2)}, u32[]{:S(2)}) %collective-permute-start.6) | collective-permute-done | bytes 131104 | tf_op jit(solution)/shard_map/ppermute | solution.py:21
  109.5 2.3 collective-permute-start.7
  111.9 8.7 %collective-permute-done.7 = bf16[4,128,128]{1,2,0:T(8,128)(2,1)S(1)} collective-permute-done((bf16[4,128,128]{1,2,0:T(8,128)(2,1)S(1)}, bf16[4,128,128]{1,2,0:T(8,128)(2,1)S(1)}, u32[]{:S(2)}, u32[]{:S(2)}) %collective-permute-start.7) | collective-permute-done | bytes 131104 | tf_op jit(solution)/shard_map/ppermute | solution.py:21
  134.8 1.0 fusion.120
  138.3 0.8 fusion.7
  139.9 0.8 fusion.9
  157.4 317.5 %all-reduce.2.cloned.1.call-done = f32[8,128,128]{1,2,0:T(8,128)} async-done(((f32[8,128,128]{1,2,0:T(8,128)}), f32[8,128,128]{1,2,0:T(8,128)}) %all-reduce.2.cloned.1.call-update) | async-done | bytes 524304 | tf_op jit(solution)/shard_map/psum | solution.py:125
  474.9 1.2 multiply_reduce_fusion
  476.5 1.0 fusion.3
  (129 shorter events, 63.7 us)
Async XLA Ops:
  6.5 1.1 copy-start
  6.5 468.4 %all-reduce.2.cloned.1.call-start = ((), (), s32[]{:S(2)}) async-start(), calls=%async_computation | async-start | bytes 1048576 | tf_op jit(solution)/shard_map/psum | solution.py:125
  9.0 12.2 %collective-permute-start = (bf16[4,128,128]{1,2,0:T(8,128)(2,1)S(1)}, bf16[4,128,128]{1,2,0:T(8,128)(2,1)S(1)}, u32[]{:S(2)}, u32[]{:S(2)}) collective-permute-start(bf16[4,128,128]{1,2,0:T(8,128)(2,1)S(1)} %copy_bitcast_fusion), channel_id=1, source_target_pairs={{480,0},{0,32},{32,64},{64,96},{96,128},{128,160},{160,192},{192,2... | collective-permute-start | bytes 393224 | tf_op jit(solution)/shard_map/ppermute | solution.py:21
  13.7 0.7 copy-start.2
  18.5 1.3 copy-start.3
  24.0 11.2 %collective-permute-start.1 = (bf16[4,128,128]{1,2,0:T(8,128)(2,1)S(1)}, bf16[4,128,128]{1,2,0:T(8,128)(2,1)S(1)}, u32[]{:S(2)}, u32[]{:S(2)}) collective-permute-start(bf16[4,128,128]{1,2,0:T(8,128)(2,1)S(1)} %collective-permute-done), channel_id=1, source_target_pairs={{480,0},{0,32},{32,64},{64,96},{96,128},{128,160},{160,192},{192,2... | collective-permute-start | bytes 393224 | tf_op jit(solution)/shard_map/ppermute | solution.py:21
  38.1 11.1 %collective-permute-start.2 = (bf16[4,128,128]{1,2,0:T(8,128)(2,1)S(1)}, bf16[4,128,128]{1,2,0:T(8,128)(2,1)S(1)}, u32[]{:S(2)}, u32[]{:S(2)}) collective-permute-start(bf16[4,128,128]{1,2,0:T(8,128)(2,1)S(1)} %collective-permute-done.1), channel_id=1, source_target_pairs={{480,0},{0,32},{32,64},{64,96},{96,128},{128,160},{160,192},{192,2... | collective-permute-start | bytes 393224 | tf_op jit(solution)/shard_map/ppermute | solution.py:21
  52.0 12.6 %collective-permute-start.3 = (bf16[4,128,128]{1,2,0:T(8,128)(2,1)S(1)}, bf16[4,128,128]{1,2,0:T(8,128)(2,1)S(1)}, u32[]{:S(2)}, u32[]{:S(2)}) collective-permute-start(bf16[4,128,128]{1,2,0:T(8,128)(2,1)S(1)} %collective-permute-done.2), channel_id=1, source_target_pairs={{480,0},{0,32},{32,64},{64,96},{96,128},{128,160},{160,192},{192,2... | collective-permute-start | bytes 393224 | tf_op jit(solution)/shard_map/ppermute | solution.py:21
  67.5 11.2 %collective-permute-start.4 = (bf16[4,128,128]{1,2,0:T(8,128)(2,1)S(1)}, bf16[4,128,128]{1,2,0:T(8,128)(2,1)S(1)}, u32[]{:S(2)}, u32[]{:S(2)}) collective-permute-start(bf16[4,128,128]{1,2,0:T(8,128)(2,1)S(1)} %collective-permute-done.3), channel_id=1, source_target_pairs={{480,0},{0,32},{32,64},{64,96},{96,128},{128,160},{160,192},{192,2... | collective-permute-start | bytes 393224 | tf_op jit(solution)/shard_map/ppermute | solution.py:21
  81.6 11.1 %collective-permute-start.5 = (bf16[4,128,128]{1,2,0:T(8,128)(2,1)S(1)}, bf16[4,128,128]{1,2,0:T(8,128)(2,1)S(1)}, u32[]{:S(2)}, u32[]{:S(2)}) collective-permute-start(bf16[4,128,128]{1,2,0:T(8,128)(2,1)S(1)} %collective-permute-done.4), channel_id=1, source_target_pairs={{480,0},{0,32},{32,64},{64,96},{96,128},{128,160},{160,192},{192,2... | collective-permute-start | bytes 393224 | tf_op jit(solution)/shard_map/ppermute | solution.py:21
  95.5 11.1 %collective-permute-start.6 = (bf16[4,128,128]{1,2,0:T(8,128)(2,1)S(1)}, bf16[4,128,128]{1,2,0:T(8,128)(2,1)S(1)}, u32[]{:S(2)}, u32[]{:S(2)}) collective-permute-start(bf16[4,128,128]{1,2,0:T(8,128)(2,1)S(1)} %collective-permute-done.5), channel_id=1, source_target_pairs={{480,0},{0,32},{32,64},{64,96},{96,128},{128,160},{160,192},{192,2... | collective-permute-start | bytes 393224 | tf_op jit(solution)/shard_map/ppermute | solution.py:21
  109.5 11.1 %collective-permute-start.7 = (bf16[4,128,128]{1,2,0:T(8,128)(2,1)S(1)}, bf16[4,128,128]{1,2,0:T(8,128)(2,1)S(1)}, u32[]{:S(2)}, u32[]{:S(2)}) collective-permute-start(bf16[4,128,128]{1,2,0:T(8,128)(2,1)S(1)} %collective-permute-done.6), channel_id=1, source_target_pairs={{480,0},{0,32},{32,64},{64,96},{96,128},{128,160},{160,192},{192,2... | collective-permute-start | bytes 393224 | tf_op jit(solution)/shard_map/ppermute | solution.py:21
  156.6 0.8 copy-start.1
  156.6 0.8 copy-start.4
Sparse Core Ops, SparseCore 0:
  157.5 317.3 all-reduce.1
where the time goes:
time: 492 us; the launch traced here: 485 us
  waiting for transfers between devices  376 us (76%)
  matrix products  54 us (11%)
  starting transfers between devices  21.9 us (4%)
  other arithmetic  15.2 us (3%)
  between operations  14.3 us (3%)
    psum x1, waiting for transfers between devices, shards(): summed = lax.psum(partials, 'tm')  317 us
    ppermute x8, waiting for transfers between devices, passed_along(): return lax.ppermute(block, axis, route)  58.8 us
    unnamed x36, matrix products  24.8 us
    ppermute x8, starting transfers between devices, passed_along(): return lax.ppermute(block, axis, route)  21.9 us
  transfers between devices with their start and end apart: 9, of which 8 were waited for; matrix products, arithmetic and copies ran while one was open for 2% of the time, Pallas kernels for 0%

commit v1 on v0

v1 whole, which is shorter than its diff:
```python
import math

import jax
import jax.numpy as jnp
import ml_dtypes
import numpy as np
from jax import lax
from jax.experimental import pallas as pl
from jax.experimental.pallas import tpu as pltpu
from jax.sharding import Mesh
from jax.sharding import PartitionSpec as P

BAND = 64
SMOOTH = 16
OFFSETS = 128
LAGS = 128
WATER = 0.1
CHANNELS = 128
SAMPLES = 512
PADDED = 256
WINDOWS = 4
BLOCKS = 16
GROUPS = 32
SPAN = 8
PLANE_GROUPS = 4
CHUNK = 10
EXTENDED = BLOCKS + SPAN

CHAN = ("x", "yh", "core")
TM = ("z", "yl")
PLANE = ("yl",) + CHAN
WHOLE = TM + CHAN
F32 = jnp.float32
BF16 = jnp.bfloat16


def angles(left, right, period):
    return 2.0 * np.pi / period * ((left[:, None] * right[None, :]) % period)


def split_table(table):
    table = table.astype(np.float32)
    high = table.astype(ml_dtypes.bfloat16)
    low = (table - high.astype(np.float32)).astype(ml_dtypes.bfloat16)
    return high, low


def band_table():
    turn = angles(np.arange(BAND) + 1, np.arange(SAMPLES), SAMPLES)
    high, low = split_table(np.concatenate([np.cos(turn), -np.sin(turn)], axis=0))
    return np.concatenate([high, low], axis=0)


def smooth_table():
    source = np.arange(BAND)[None, :]
    start = np.clip(np.arange(BAND)[:, None] - SMOOTH // 2, 0, BAND - SMOOTH)
    inside = (source >= start) & (source < start + SMOOTH)
    return np.concatenate([inside, np.ones_like(inside)], axis=0).astype(ml_dtypes.bfloat16)


def channel_table():
    turn = angles(np.arange(CHANNELS), np.arange(PADDED), PADDED)
    top = np.concatenate([np.cos(turn), -np.sin(turn)], axis=1)
    bottom = np.concatenate([np.sin(turn), np.cos(turn)], axis=1)
    return split_table(np.concatenate([top, bottom], axis=0))


def offset_table():
    turn = angles(np.arange(PADDED), np.arange(OFFSETS) - OFFSETS // 2, PADDED)
    top = np.concatenate([np.cos(turn), np.sin(turn)], axis=1)
    bottom = np.concatenate([-np.sin(turn), np.cos(turn)], axis=1)
    return split_table(np.concatenate([top, bottom], axis=0) / PADDED)


def lag_table():
    turn = angles(np.arange(BAND) + 1, np.arange(LAGS) - LAGS // 2, SAMPLES)
    pair = np.stack([np.cos(turn), -np.sin(turn)], axis=1).reshape(2 * BAND, LAGS)
    return split_table(pair / math.sqrt(BAND))


def dot(left, right):
    return jnp.dot(left, right, preferred_element_type=F32)


def split(value):
    high = value.astype(BF16)
    return high, (value - high.astype(F32)).astype(BF16)


def dot_split(value, table_high, table_low):
    high, low = split(value)
    return dot(high, table_high) + (dot(low, table_high) + dot(high, table_low))


def whiten_kernel(place, owners, counts, traces, table, smooth, out, rows):
    flat = traces[...].reshape(WINDOWS * CHANNELS, SAMPLES)
    both = lax.dot_general(
        table[...], flat, (((1,), (1,)), ((), ())), preferred_element_type=F32
    )
    spectrum = both[: 2 * BAND] + both[2 * BAND :]
    real_part = spectrum[:BAND]
    imag_part = spectrum[BAND:]
    amplitude = jnp.sqrt(real_part * real_part + imag_part * imag_part)
    high, low = split(amplitude)
    sums = dot(smooth[...], high) + dot(smooth[...], low)
    water_level = sums[:BAND] / SMOOTH + WATER * (sums[BAND:] / BAND) + 1e-6
    real_part = real_part / water_level
    imag_part = imag_part / water_level
    for window in range(WINDOWS):
        here = slice(window * CHANNELS, (window + 1) * CHANNELS)
        rows[pl.ds(window, BAND, stride=CHUNK), :] = real_part[:, here]
        rows[pl.ds(WINDOWS + window, BAND, stride=CHUNK), :] = imag_part[:, here]
    lane = lax.broadcasted_iota(jnp.int32, (8, CHANNELS), 1)
    count_row = jnp.zeros((8, CHANNELS), jnp.int32)
    owner_row = jnp.zeros((8, CHANNELS), jnp.int32)
    for step in range(SPAN):
        count_row = jnp.where(lane == step, counts[step, place[0]], count_row)
        owner_row = jnp.where(lane == step, owners[0, step], owner_row)
    count_row = count_row.astype(F32)
    owner_row = owner_row.astype(F32)
    for part in range(BAND // 8):
        rows[pl.ds(part * 8 * CHUNK + 8, 8, stride=CHUNK), :] = count_row
        rows[pl.ds(part * 8 * CHUNK + 9, 8, stride=CHUNK), :] = owner_row
    out[...] = rows[...].astype(BF16)


def cross_kernel(
    chunks, to_high, to_low, back_high, back_low, out, rows, stacked, spectra, cross, slots
):
    rows[...] = chunks[...].astype(F32)
    block_rows = BLOCKS * CHUNK
    for group in range(PLANE_GROUPS):
        for window in range(WINDOWS):
            base = (group * WINDOWS + window) * EXTENDED
            for part in range(2):
                start = group * block_rows + part * WINDOWS + window
                lanes = slice(part * CHANNELS, (part + 1) * CHANNELS)
                stacked[base : base + 8, lanes] = rows[
                    pl.ds(start + 8 * CHUNK, 8, stride=CHUNK), :
                ]
                stacked[base + 8 : base + 24, lanes] = rows[pl.ds(start, 16, stride=CHUNK), :]
    block_data = stacked[...].astype(BF16)
    both = dot(block_data, to_high[...]) + dot(block_data, to_low[...])
    for tile in range(4):
        spectra[tile] = both[:, tile * 128 : (tile + 1) * 128]
    counts = [
        rows[pl.ds(group * block_rows + 8, 16, stride=CHUNK), :] for group in range(PLANE_GROUPS)
    ]
    owners = rows[pl.ds(9, 16, stride=CHUNK), :]
    for step in range(SPAN):
        distance = step + 1
        limits = [
            jnp.broadcast_to(counts[group][:, step : step + 1], (BLOCKS, 128))
            for group in range(PLANE_GROUPS)
        ]
        for half in range(2):
            total_real = jnp.zeros((BLOCKS, 128), F32)
            total_imag = jnp.zeros((BLOCKS, 128), F32)
            for group in range(PLANE_GROUPS):
                for window in range(WINDOWS):
                    base = (group * WINDOWS + window) * EXTENDED + SPAN
                    own = slice(base, base + BLOCKS)
                    before = slice(base - distance, base - distance + BLOCKS)
                    own_real = spectra[half, own, :]
                    own_imag = spectra[2 + half, own, :]
                    src_real = spectra[half, before, :]
                    src_imag = spectra[2 + half, before, :]
                    term_real = src_real * own_real + src_imag * own_imag
                    term_imag = src_real * own_imag - src_imag * own_real
                    keep = limits[group] > float(window)
                    total_real = total_real + jnp.where(keep, term_real, 0.0)
                    total_imag = total_imag + jnp.where(keep, term_imag, 0.0)
            here = slice(step * BLOCKS, (step + 1) * BLOCKS)
            cross[here, half * 128 : (half + 1) * 128] = total_real
            cross[here, PADDED + half * 128 : PADDED + (half + 1) * 128] = total_imag
    partial = dot_split(cross[...], back_high[...], back_low[...])
    owner_of = [
        jnp.broadcast_to(owners[:, step : step + 1], (BLOCKS, 128)) for step in range(SPAN)
    ]
    for owner in range(GROUPS):
        halves = [jnp.zeros((BLOCKS, 128), F32), jnp.zeros((BLOCKS, 128), F32)]
        for step in range(SPAN):
            chosen = owner_of[step] == float(owner)
            for half in range(2):
                piece = partial[
                    step * BLOCKS : (step + 1) * BLOCKS, half * 128 : (half + 1) * 128
                ]
                halves[half] = jnp.where(chosen, piece, halves[half])
        for half in range(2):
            slots[pl.ds(owner * 2 * BLOCKS + half, BLOCKS, stride=2), :] = halves[half]
    out[...] = slots[...].astype(BF16)


def lag_kernel(place, listed, owners, counts, arrived, table_high, table_low, out):
    mine = jnp.int32(0)
    found = jnp.int32(0)
    for step in range(SPAN):
        here = owners[0, step] == place[0]
        mine = jnp.where(here, step, mine)
        found = jnp.where(here, listed[0, step], found)
    total = jnp.int32(0)
    for group in range(GROUPS):
        total = total + counts[mine, group]
    weight = jnp.full((8, LAGS), found, jnp.int32).astype(F32) / jnp.full(
        (8, LAGS), total, jnp.int32
    ).astype(F32)
    summed = arrived[: 2 * BAND].astype(F32)
    for layer in range(1, 8):
        summed = summed + arrived[layer * 2 * BAND : (layer + 1) * 2 * BAND].astype(F32)
    lagged = dot_split(summed.T, table_high[...], table_low[...])
    out[...] = lagged * weight[:1]


def shards(traces, pair_listed, owner_slot, window_count):
    vmem = pl.BlockSpec(memory_space=pltpu.VMEM)
    smem = pl.BlockSpec(memory_space=pltpu.SMEM)
    place = lax.axis_index(TM).astype(jnp.int32).reshape(1)
    counts = window_count[0]
    chunks = pl.pallas_call(
        whiten_kernel,
        out_shape=jax.ShapeDtypeStruct((BAND * CHUNK, CHANNELS), BF16),
        in_specs=[smem, smem, smem, vmem, vmem, vmem],
        out_specs=vmem,
        scratch_shapes=[pltpu.VMEM((BAND * CHUNK, CHANNELS), F32)],
        compiler_params=pltpu.CompilerParams(vmem_limit_bytes=32 << 20),
        name="whiten",
    )(place, owner_slot, counts, traces[0], band_table(), smooth_table())
    chunks = chunks.reshape(BAND, CHUNK // 2, 2, CHANNELS)
    chunks = lax.all_to_all(chunks, PLANE, 0, 0, tiled=True)
    chunks = chunks.reshape(BAND * CHUNK, CHANNELS)
    slots = pl.pallas_call(
        cross_kernel,
        out_shape=jax.ShapeDtypeStruct((GROUPS * BLOCKS * 2, OFFSETS), BF16),
        in_specs=[vmem] * 5,
        out_specs=vmem,
        scratch_shapes=[
            pltpu.VMEM((BAND * CHUNK, CHANNELS), F32),
            pltpu.VMEM((PLANE_GROUPS * WINDOWS * EXTENDED, 2 * CHANNELS), F32),
            pltpu.VMEM((4, PLANE_GROUPS * WINDOWS * EXTENDED, 128), F32),
            pltpu.VMEM((SPAN * BLOCKS, 2 * PADDED), F32),
            pltpu.VMEM((GROUPS * BLOCKS * 2, OFFSETS), F32),
        ],
        compiler_params=pltpu.CompilerParams(vmem_limit_bytes=32 << 20),
        name="cross",
    )(chunks, *channel_table(), *offset_table())
    slots = slots.reshape(GROUPS * BLOCKS, 2, OFFSETS)
    slots = lax.all_to_all(slots, WHOLE, 0, 0, tiled=True)
    slots = slots.reshape(GROUPS * BLOCKS * 2, OFFSETS)
    stacked = pl.pallas_call(
        lag_kernel,
        out_shape=jax.ShapeDtypeStruct((OFFSETS, LAGS), F32),
        in_specs=[smem, smem, smem, smem, vmem, vmem, vmem],
        out_specs=vmem,
        compiler_params=pltpu.CompilerParams(vmem_limit_bytes=32 << 20),
        name="lag",
    )(place, pair_listed, owner_slot, counts, slots, *lag_table())
    return stacked[None, None]


def solution(mesh):
    fine = Mesh(mesh.devices.reshape(4, 2, 2, 8, 4), CHAN + TM)
    placed = (
        P(CHAN, TM, None, None),
        P(CHAN, None),
        P(CHAN, None),
        P(CHAN, None, None),
    )
    return jax.shard_map(
        shards, mesh=fine, in_specs=placed, out_specs=P(CHAN, TM, None, None), check_vma=False
    )
```

time: 492 us -> 63.5 us (0.13)
  the two profiles are of different devices: /device:TPU:2 before, /device:TPU:1 now
where the time goes in v1:
time: 63.5 us; the launch traced here: 63.1 us
  blocking collectives  54.5 us (86%)
  Pallas kernels  4.42 us (7%)
  local copies, waits for them, and re-layouts  4.12 us (6%)
    all_to_all x1, blocking collectives, shards(): slots = lax.all_to_all(slots, WHOLE, 0, 0, tiled=True)  31.4 us
    all_to_all x1, blocking collectives, shards(): chunks = lax.all_to_all(chunks, PLANE, 0, 0, tiled=True)  23.1 us
    unnamed x26, local copies, waits for them, and re-layouts  4.12 us
    pallas_call x1, Pallas kernels, shards(): pl.pallas_call(cross_kernel, out_shape=jax.ShapeDtypeStruct((GROUPS * BLO...  1.73 us
    pallas_call x1, Pallas kernels, shards(): pl.pallas_call(lag_kernel, out_shape=jax.ShapeDtypeStruct((OFFSETS, LAGS)...  1.48 us

profile of v1, /device:TPU:1, one launch (start us, length us, event | category | flops | bytes accessed | tf_op | source)
XLA Modules:
  0.0 63.1 jit_solution(17308523182118830261)
XLA Ops:
  0.0 0.0 copy-start.8
  0.0 0.0 copy-start.11
  0.0 0.8 %copy-done.8 = bf16[128,64]{1,0:T(8,128)(2,1)S(1)} copy-done((bf16[128,64]{1,0:T(8,128)(2,1)S(1)}, bf16[128,64]{1,0:T(8,128)(2,1)}, u32[]{:S(2)}) %copy-start.8) | copy-done | bytes 16408
  0.8 0.0 copy-done.11
  0.8 1.0 %copy-done = bf16[1,4,128,512]{3,2,1,0:T(8,128)(2,1)S(1)} copy-done((bf16[1,4,128,512]{3,2,1,0:T(8,128)(2,1)S(1)}, bf16[1,4,128,512]{3,2,1,0:T(8,128)(2,1)}, u32[]{:S(2)}) %copy-start) | copy-done | bytes 524312
  1.8 0.9 %copy-done.1 = bf16[256,512]{1,0:T(8,128)(2,1)S(1)} copy-done((bf16[256,512]{1,0:T(8,128)(2,1)S(1)}, bf16[256,512]{1,0:T(8,128)(2,1)}, u32[]{:S(2)}) %copy-start.1) | copy-done | bytes 262168
  2.8 0.7 %copy-done.9 = s32[1,8,32]{2,1,0:T(8,128)S(1)} copy-done((s32[1,8,32]{2,1,0:T(8,128)S(1)}, s32[1,8,32]{2,1,0:T(8,128)}, u32[]{:S(2)}) %copy-start.9) | copy-done | bytes 1048
  3.4 1.2 %whiten.1 = bf16[640,128]{1,0:T(8,128)(2,1)S(1)} custom-call(s32[1]{0:T(128)} %bitcast.place, s32[1,8]{1,0:T(1,128)S(1)} %copy-done.11, s32[8,32]{1,0:T(8,128)S(1)} %bitcast.13, bf16[4,128,512]{2,1,0:T(8,128)(2,1)S(1)} %bitcast.12, bf16[256,512]{1,0:T(8,128)(2,1)S(1)} %copy-done.1, bf16[128,64]{1,0:T(8,128)(2,1)S(1)} %copy-done.8), custom_call_target="tpu_custom_call" | custom-call | tf_op jit(solution)/shard_map/whiten/pallas_call | solution.py:219
  4.7 0.0 copy-start.2
  4.7 23.1 %all_to_all.10 = bf16[64,5,2,128]{3,2,1,0:T(2,128)(2,1)S(1)} all-to-all(bf16[64,5,2,128]{3,2,1,0:T(2,128)(2,1)S(1)} %bitcast.10), channel_id=1, replica_groups=mesh['x'=4,'yh'=2,'core'=2,'z'=8,'yl'=4] {'yl','x','yh','core'}, dimensions={0} | all-to-all | bytes 327680 | tf_op jit(solution)/shard_map/all_to_all | solution.py:229
  27.8 0.0 copy-done.3
  27.8 0.0 copy-done.4
  27.8 0.0 copy-done.5
  27.8 0.0 copy-done.2
  27.8 1.7 %cross.1 = bf16[1024,128]{1,0:T(8,128)(2,1)S(1)} custom-call(bf16[640,128]{1,0:T(8,128)(2,1)S(1)} %bitcast.11, bf16[256,512]{1,0:T(8,128)(2,1)S(1)} %copy-done.5, bf16[256,512]{1,0:T(8,128)(2,1)S(1)} %copy-done.4, bf16[512,256]{1,0:T(8,128)(2,1)S(1)} %copy-done.3, bf16[512,256]{1,0:T(8,128)(2,1)S(1)} %copy-done.2), custom_call_target="tpu_custom_call" | custom-call | tf_op jit(solution)/shard_map/cross/pallas_call | solution.py:231
  29.6 0.0 copy-start.6
  29.6 0.0 copy-start.7
  29.6 0.0 copy-start.10
  29.6 31.4 %all_to_all.11 = bf16[512,2,128]{2,1,0:T(2,128)(2,1)S(1)} all-to-all(bf16[512,2,128]{2,1,0:T(2,128)(2,1)S(1)} %bitcast.9), channel_id=1, replica_groups=mesh['x'=4,'yh'=2,'core'=2,'z'=8,'yl'=4] {'z','yl','x','yh','core'}, dimensions={0} | all-to-all | bytes 524288 | tf_op jit(solution)/shard_map/all_to_all | solution.py:247
  61.0 0.0 copy-done.6
  61.0 0.0 copy-done.7
  61.0 0.0 copy-done.10
  61.0 0.6 %copy-done.12 = s32[1,8]{1,0:T(1,128)S(1)} copy-done((s32[1,8]{1,0:T(1,128)S(1)}, s32[1,8]{1,0:T(1,128)}, u32[]{:S(2)}) %copy-start.12) | copy-done | bytes 56
  61.7 1.5 %lag.1 = f32[128,128]{1,0:T(8,128)} custom-call(s32[1]{0:T(128)} %bitcast.place, s32[1,8]{1,0:T(1,128)S(1)} %copy-done.12, s32[1,8]{1,0:T(1,128)S(1)} %copy-done.11, s32[8,32]{1,0:T(8,128)S(1)} %bitcast.14, bf16[1024,128]{1,0:T(8,128)(2,1)S(1)} %bitcast.8, bf16[128,128]{1,0:T(8,128)(2,1)S(1)} %copy-done.7, bf16[128,128]{1,0:T(8,128)(2,1)S(1)} %copy-done.6), custom_call_target="tpu_custom_call" | custom-call | tf_op jit(solution)/shard_map/lag/pallas_call | solution.py:249
  (7 shorter events, 0.0 us)
Async XLA Ops:
  0.0 0.8 %copy-start.8 = (bf16[128,64]{1,0:T(8,128)(2,1)S(1)}, bf16[128,64]{1,0:T(8,128)(2,1)}, u32[]{:S(2)}) copy-start(bf16[128,64]{1,0:T(8,128)(2,1)} %constant.28.clone.smooth) | copy-start | bytes 49156
  0.0 0.8 %copy-start.11 = (s32[1,8]{1,0:T(1,128)S(1)}, s32[1,8]{1,0:T(1,128)}, u32[]{:S(2)}) copy-start(s32[1,8]{1,0:T(1,128)} %owners.3) | copy-start | bytes 100
  0.8 1.0 %copy-start = (bf16[1,4,128,512]{3,2,1,0:T(8,128)(2,1)S(1)}, bf16[1,4,128,512]{3,2,1,0:T(8,128)(2,1)}, u32[]{:S(2)}) copy-start(bf16[1,4,128,512]{3,2,1,0:T(8,128)(2,1)} %param.12) | copy-start | bytes 1572868
  1.8 0.9 %copy-start.1 = (bf16[256,512]{1,0:T(8,128)(2,1)S(1)}, bf16[256,512]{1,0:T(8,128)(2,1)}, u32[]{:S(2)}) copy-start(bf16[256,512]{1,0:T(8,128)(2,1)} %constant.27.clone.table) | copy-start | bytes 786436
  2.8 0.7 %copy-start.9 = (s32[1,8,32]{2,1,0:T(8,128)S(1)}, s32[1,8,32]{2,1,0:T(8,128)}, u32[]{:S(2)}) copy-start(s32[1,8,32]{2,1,0:T(8,128)} %param.15) | copy-start | bytes 3076
  3.4 24.4 %copy-start.3 = (bf16[512,256]{1,0:T(8,128)(2,1)S(1)}, bf16[512,256]{1,0:T(8,128)(2,1)}, u32[]{:S(2)}) copy-start(bf16[512,256]{1,0:T(8,128)(2,1)} %constant.31.clone.back_high) | copy-start | bytes 786436
  3.4 24.4 %copy-start.4 = (bf16[256,512]{1,0:T(8,128)(2,1)S(1)}, bf16[256,512]{1,0:T(8,128)(2,1)}, u32[]{:S(2)}) copy-start(bf16[256,512]{1,0:T(8,128)(2,1)} %constant.30.clone.to_low) | copy-start | bytes 786436
  3.4 24.4 %copy-start.5 = (bf16[256,512]{1,0:T(8,128)(2,1)S(1)}, bf16[256,512]{1,0:T(8,128)(2,1)}, u32[]{:S(2)}) copy-start(bf16[256,512]{1,0:T(8,128)(2,1)} %constant.29.clone.to_high) | copy-start | bytes 786436
  4.7 23.2 %copy-start.2 = (bf16[512,256]{1,0:T(8,128)(2,1)S(1)}, bf16[512,256]{1,0:T(8,128)(2,1)}, u32[]{:S(2)}) copy-start(bf16[512,256]{1,0:T(8,128)(2,1)} %constant.32.clone.back_low) | copy-start | bytes 786436
  29.6 31.4 %copy-start.6 = (bf16[128,128]{1,0:T(8,128)(2,1)S(1)}, bf16[128,128]{1,0:T(8,128)(2,1)}, u32[]{:S(2)}) copy-start(bf16[128,128]{1,0:T(8,128)(2,1)} %constant.34.clone.table_low) | copy-start | bytes 98308
  29.6 31.4 %copy-start.7 = (bf16[128,128]{1,0:T(8,128)(2,1)S(1)}, bf16[128,128]{1,0:T(8,128)(2,1)}, u32[]{:S(2)}) copy-start(bf16[128,128]{1,0:T(8,128)(2,1)} %constant.33.clone.table_high) | copy-start | bytes 98308
  29.6 31.4 %copy-start.10 = (s32[1,8,32]{2,1,0:T(8,128)S(1)}, s32[1,8,32]{2,1,0:T(8,128)}, u32[]{:S(2)}) copy-start(s32[1,8,32]{2,1,0:T(8,128)} %param.15) | copy-start | bytes 3076
  61.0 0.7 %copy-start.12 = (s32[1,8]{1,0:T(1,128)S(1)}, s32[1,8]{1,0:T(1,128)}, u32[]{:S(2)}) copy-start(s32[1,8]{1,0:T(1,128)} %listed.1) | copy-start | bytes 100

commit v2 on v1

--- a/solution.py
+++ b/solution.py
@@ -51,13 +51,6 @@
     return np.concatenate([high, low], axis=0)
 
 
-def smooth_table():
-    source = np.arange(BAND)[None, :]
-    start = np.clip(np.arange(BAND)[:, None] - SMOOTH // 2, 0, BAND - SMOOTH)
-    inside = (source >= start) & (source < start + SMOOTH)
-    return np.concatenate([inside, np.ones_like(inside)], axis=0).astype(ml_dtypes.bfloat16)
-
-
 def channel_table():
     turn = angles(np.arange(CHANNELS), np.arange(PADDED), PADDED)
     top = np.concatenate([np.cos(turn), -np.sin(turn)], axis=1)
@@ -92,7 +85,80 @@
     return dot(high, table_high) + (dot(low, table_high) + dot(high, table_low))
 
 
-def whiten_kernel(place, owners, counts, traces, table, smooth, out, rows):
+def smooth_sums(amplitude):
+    target = lax.broadcasted_iota(jnp.int32, (2 * BAND, BAND), 0)
+    source = lax.broadcasted_iota(jnp.int32, (2 * BAND, BAND), 1)
+    start = jnp.clip(target - SMOOTH // 2, 0, BAND - SMOOTH)
+    inside = (target >= BAND) | ((source >= start) & (source < start + SMOOTH))
+    smooth = inside.astype(F32).astype(BF16)
+    high, low = split(amplitude)
+    sums = dot(smooth, high) + dot(smooth, low)
+    return sums[:BAND], sums[BAND:]
+
+
+def whiten_kernel(
+    place,
+    listed_hbm,
+    owners_hbm,
+    counts_hbm,
+    traces_hbm,
+    table_hbm,
+    out,
+    weight,
+    listed,
+    owners,
+    counts,
+    traces,
+    table,
+    rows,
+    small_sems,
+    table_sem,
+    trace_sems,
+):
+    small = [
+        pltpu.make_async_copy(source, target, small_sems.at[k])
+        for k, (source, target) in enumerate(
+            ((listed_hbm, listed), (owners_hbm, owners), (counts_hbm, counts))
+        )
+    ]
+    whole_table = pltpu.make_async_copy(table_hbm, table, table_sem)
+    parts = [
+        pltpu.make_async_copy(traces_hbm.at[window], traces.at[window], trace_sems.at[window])
+        for window in range(WINDOWS)
+    ]
+    whole_table.start()
+    for copy in parts:
+        copy.start()
+    for copy in small:
+        copy.start()
+    for copy in small:
+        copy.wait()
+    lane = lax.broadcasted_iota(jnp.int32, (8, CHANNELS), 1)
+    count_row = jnp.zeros((8, CHANNELS), jnp.int32)
+    owner_row = jnp.zeros((8, CHANNELS), jnp.int32)
+    mine = jnp.int32(0)
+    found = jnp.int32(0)
+    for step in range(SPAN):
+        owner = owners[0, step]
+        count_row = jnp.where(lane == step, counts[step, place[0]], count_row)
+        owner_row = jnp.where(lane == step, owner, owner_row)
+        here = owner == place[0]
+        mine = jnp.where(here, step, mine)
+        found = jnp.where(here, listed[0, step], found)
+    total = jnp.int32(0)
+    for group in range(GROUPS):
+        total = total + counts[mine, group]
+    weight[...] = jnp.full((8, LAGS), found, jnp.int32).astype(F32) / jnp.full(
+        (8, LAGS), total, jnp.int32
+    ).astype(F32)
+    count_row = count_row.astype(F32)
+    owner_row = owner_row.astype(F32)
+    for part in range(BAND // 8):
+        rows[pl.ds(part * 8 * CHUNK + 8, 8, stride=CHUNK), :] = count_row
+        rows[pl.ds(part * 8 * CHUNK + 9, 8, stride=CHUNK), :] = owner_row
+    whole_table.wait()
+    for copy in parts:
+        copy.wait()
     flat = traces[...].reshape(WINDOWS * CHANNELS, SAMPLES)
     both = lax.dot_general(
         table[...], flat, (((1,), (1,)), ((), ())), preferred_element_type=F32
@@ -101,26 +167,14 @@
     real_part = spectrum[:BAND]
     imag_part = spectrum[BAND:]
     amplitude = jnp.sqrt(real_part * real_part + imag_part * imag_part)
-    high, low = split(amplitude)
-    sums = dot(smooth[...], high) + dot(smooth[...], low)
-    water_level = sums[:BAND] / SMOOTH + WATER * (sums[BAND:] / BAND) + 1e-6
+    near, everywhere = smooth_sums(amplitude)
+    water_level = near / SMOOTH + WATER * (everywhere / BAND) + 1e-6
     real_part = real_part / water_level
     imag_part = imag_part / water_level
     for window in range(WINDOWS):
         here = slice(window * CHANNELS, (window + 1) * CHANNELS)
         rows[pl.ds(window, BAND, stride=CHUNK), :] = real_part[:, here]
         rows[pl.ds(WINDOWS + window, BAND, stride=CHUNK), :] = imag_part[:, here]
-    lane = lax.broadcasted_iota(jnp.int32, (8, CHANNELS), 1)
-    count_row = jnp.zeros((8, CHANNELS), jnp.int32)
-    owner_row = jnp.zeros((8, CHANNELS), jnp.int32)
-    for step in range(SPAN):
-        count_row = jnp.where(lane == step, counts[step, place[0]], count_row)
-        owner_row = jnp.where(lane == step, owners[0, step], owner_row)
-    count_row = count_row.astype(F32)
-    owner_row = owner_row.astype(F32)
-    for part in range(BAND // 8):
-        rows[pl.ds(part * 8 * CHUNK + 8, 8, stride=CHUNK), :] = count_row
-        rows[pl.ds(part * 8 * CHUNK + 9, 8, stride=CHUNK), :] = owner_row
     out[...] = rows[...].astype(BF16)
 
 
@@ -131,18 +185,23 @@
     block_rows = BLOCKS * CHUNK
     for group in range(PLANE_GROUPS):
         for window in range(WINDOWS):
-            base = (group * WINDOWS + window) * EXTENDED
+            base = (group * WINDOWS + window) * BLOCKS
             for part in range(2):
                 start = group * block_rows + part * WINDOWS + window
                 lanes = slice(part * CHANNELS, (part + 1) * CHANNELS)
-                stacked[base : base + 8, lanes] = rows[
-                    pl.ds(start + 8 * CHUNK, 8, stride=CHUNK), :
+                stacked[base : base + BLOCKS, lanes] = rows[
+                    pl.ds(start, BLOCKS, stride=CHUNK), :
                 ]
-                stacked[base + 8 : base + 24, lanes] = rows[pl.ds(start, 16, stride=CHUNK), :]
     block_data = stacked[...].astype(BF16)
     both = dot(block_data, to_high[...]) + dot(block_data, to_low[...])
     for tile in range(4):
-        spectra[tile] = both[:, tile * 128 : (tile + 1) * 128]
+        lanes = slice(tile * 128, (tile + 1) * 128)
+        for window in range(PLANE_GROUPS * WINDOWS):
+            source, target = window * BLOCKS, window * EXTENDED
+            spectra[tile, target : target + SPAN, :] = both[source + SPAN : source + BLOCKS, lanes]
+            spectra[tile, target + SPAN : target + EXTENDED, :] = both[
+                source : source + BLOCKS, lanes
+            ]
     counts = [
         rows[pl.ds(group * block_rows + 8, 16, stride=CHUNK), :] for group in range(PLANE_GROUPS)
     ]
@@ -167,9 +226,12 @@
                     src_imag = spectra[2 + half, before, :]
                     term_real = src_real * own_real + src_imag * own_imag
                     term_imag = src_real * own_imag - src_imag * own_real
-                    keep = limits[group] > float(window)
-                    total_real = total_real + jnp.where(keep, term_real, 0.0)
-                    total_imag = total_imag + jnp.where(keep, term_imag, 0.0)
+                    if window > 0:
+                        keep = limits[group] > float(window)
+                        term_real = jnp.where(keep, term_real, 0.0)
+                        term_imag = jnp.where(keep, term_imag, 0.0)
+                    total_real = total_real + term_real
+                    total_imag = total_imag + term_imag
             here = slice(step * BLOCKS, (step + 1) * BLOCKS)
             cross[here, half * 128 : (half + 1) * 128] = total_real
             cross[here, PADDED + half * 128 : PADDED + (half + 1) * 128] = total_imag
@@ -191,19 +253,7 @@
     out[...] = slots[...].astype(BF16)
 
 
-def lag_kernel(place, listed, owners, counts, arrived, table_high, table_low, out):
-    mine = jnp.int32(0)
-    found = jnp.int32(0)
-    for step in range(SPAN):
-        here = owners[0, step] == place[0]
-        mine = jnp.where(here, step, mine)
-        found = jnp.where(here, listed[0, step], found)
-    total = jnp.int32(0)
-    for group in range(GROUPS):
-        total = total + counts[mine, group]
-    weight = jnp.full((8, LAGS), found, jnp.int32).astype(F32) / jnp.full(
-        (8, LAGS), total, jnp.int32
-    ).astype(F32)
+def lag_kernel(arrived, weight, table_high, table_low, out):
     summed = arrived[: 2 * BAND].astype(F32)
     for layer in range(1, 8):
         summed = summed + arrived[layer * 2 * BAND : (layer + 1) * 2 * BAND].astype(F32)
@@ -215,16 +265,29 @@
     vmem = pl.BlockSpec(memory_space=pltpu.VMEM)
     smem = pl.BlockSpec(memory_space=pltpu.SMEM)
     place = lax.axis_index(TM).astype(jnp.int32).reshape(1)
-    counts = window_count[0]
-    chunks = pl.pallas_call(
+    hbm = pl.BlockSpec(memory_space=pltpu.HBM)
+    chunks, weight = pl.pallas_call(
         whiten_kernel,
-        out_shape=jax.ShapeDtypeStruct((BAND * CHUNK, CHANNELS), BF16),
-        in_specs=[smem, smem, smem, vmem, vmem, vmem],
-        out_specs=vmem,
-        scratch_shapes=[pltpu.VMEM((BAND * CHUNK, CHANNELS), F32)],
-        compiler_params=pltpu.CompilerParams(vmem_limit_bytes=32 << 20),
+        out_shape=(
+            jax.ShapeDtypeStruct((BAND * CHUNK, CHANNELS), BF16),
+            jax.ShapeDtypeStruct((8, LAGS), F32),
+        ),
+        in_specs=[smem, hbm, hbm, hbm, hbm, hbm],
+        out_specs=(vmem, vmem),
+        scratch_shapes=[
+            pltpu.SMEM((1, SPAN), jnp.int32),
+            pltpu.SMEM((1, SPAN), jnp.int32),
+            pltpu.SMEM((SPAN, GROUPS), jnp.int32),
+            pltpu.VMEM((WINDOWS, CHANNELS, SAMPLES), BF16),
+            pltpu.VMEM((4 * BAND, SAMPLES), BF16),
+            pltpu.VMEM((BAND * CHUNK, CHANNELS), F32),
+            pltpu.SemaphoreType.DMA((3,)),
+            pltpu.SemaphoreType.DMA,
+            pltpu.SemaphoreType.DMA((WINDOWS,)),
+        ],
+        compiler_params=pltpu.CompilerParams(vmem_limit_bytes=60 << 20),
         name="whiten",
-    )(place, owner_slot, counts, traces[0], band_table(), smooth_table())
+    )(place, pair_listed, owner_slot, window_count[0], traces[0], band_table())
     chunks = chunks.reshape(BAND, CHUNK // 2, 2, CHANNELS)
     chunks = lax.all_to_all(chunks, PLANE, 0, 0, tiled=True)
     chunks = chunks.reshape(BAND * CHUNK, CHANNELS)
@@ -235,7 +298,7 @@
         out_specs=vmem,
         scratch_shapes=[
             pltpu.VMEM((BAND * CHUNK, CHANNELS), F32),
-            pltpu.VMEM((PLANE_GROUPS * WINDOWS * EXTENDED, 2 * CHANNELS), F32),
+            pltpu.VMEM((PLANE_GROUPS * WINDOWS * BLOCKS, 2 * CHANNELS), F32),
             pltpu.VMEM((4, PLANE_GROUPS * WINDOWS * EXTENDED, 128), F32),
             pltpu.VMEM((SPAN * BLOCKS, 2 * PADDED), F32),
             pltpu.VMEM((GROUPS * BLOCKS * 2, OFFSETS), F32),
@@ -249,11 +312,11 @@
     stacked = pl.pallas_call(
         lag_kernel,
         out_shape=jax.ShapeDtypeStruct((OFFSETS, LAGS), F32),
-        in_specs=[smem, smem, smem, smem, vmem, vmem, vmem],
+        in_specs=[vmem] * 4,
         out_specs=vmem,
         compiler_params=pltpu.CompilerParams(vmem_limit_bytes=32 << 20),
         name="lag",
-    )(place, pair_listed, owner_slot, counts, slots, *lag_table())
+    )(slots, weight, *lag_table())
     return stacked[None, None]
 
 

time: 63.5 us -> 60.2 us (0.948)
  local copies, waits for them, and re-layouts: 4.12 us -> 0.04 us
  Pallas kernels: 4.42 us -> 5.13 us
    unnamed x26 -> x14, local copies, waits for them, and re-layouts: 4.12 us -> 0.04 us
    pallas_call x1, Pallas kernels: 1.22 us -> 2.59 us  [shards(): pl.pallas_call(whiten_kernel, out_shape=(jax.ShapeDtypeStruct((BAND * CHU...]
where the time goes in v2:
time: 60.2 us; the launch traced here: 60 us
  blocking collectives  54.7 us (91%)
  Pallas kernels  5.13 us (9%)
    all_to_all x1, blocking collectives, shards(): slots = lax.all_to_all(slots, WHOLE, 0, 0, tiled=True)  31.4 us
    all_to_all x1, blocking collectives, shards(): chunks = lax.all_to_all(chunks, PLANE, 0, 0, tiled=True)  23.3 us
    pallas_call x1, Pallas kernels, shards(): pl.pallas_call(whiten_kernel, out_shape=(jax.ShapeDtypeStruct((BAND * CHU...  2.59 us
    pallas_call x1, Pallas kernels, shards(): pl.pallas_call(cross_kernel, out_shape=jax.ShapeDtypeStruct((GROUPS * BLO...  1.66 us

profile of v2, /device:TPU:1, one launch (start us, length us, event | category | flops | bytes accessed | tf_op | source)
XLA Modules:
  0.0 60.0 jit_solution(14699058618170148081)
XLA Ops:
  0.0 0.0 copy-start.1
  0.0 0.0 copy-start.2
  0.0 0.0 copy-start.3
  0.0 2.6 %whiten.1 = (bf16[640,128]{1,0:T(8,128)(2,1)}, f32[8,128]{1,0:T(8,128)}) custom-call(s32[1]{0:T(128)} %bitcast.place, s32[1,8]{1,0:T(1,128)} %listed_hbm.1, s32[1,8]{1,0:T(1,128)} %owners_hbm.1, s32[8,32]{1,0:T(8,128)} %bitcast.13, bf16[4,128,512]{2,1,0:T(8,128)(2,1)} %bitcast.11, bf16[256,512]{1,0:T(8,128)(2,1)} %constant.25.clone.table_hbm), custom_call_target="tpu_custom_call" | custom-call | tf_op jit(solution)/shard_map/whiten/pallas_call | solution.py:269
  2.6 0.0 copy-start
  2.6 23.3 %all_to_all.10 = bf16[64,5,2,128]{3,2,1,0:T(2,128)(2,1)S(1)} all-to-all(bf16[64,5,2,128]{3,2,1,0:T(2,128)(2,1)} %bitcast.12), channel_id=1, replica_groups=mesh['x'=4,'yh'=2,'core'=2,'z'=8,'yl'=4] {'yl','x','yh','core'}, dimensions={0} | all-to-all | bytes 327680 | tf_op jit(solution)/shard_map/all_to_all | solution.py:292
  26.0 0.0 copy-done.1
  26.0 0.0 copy-done.2
  26.0 0.0 copy-done.3
  26.0 0.0 copy-done
  26.0 1.7 %cross.1 = bf16[1024,128]{1,0:T(8,128)(2,1)S(1)} custom-call(bf16[640,128]{1,0:T(8,128)(2,1)S(1)} %bitcast.10, bf16[256,512]{1,0:T(8,128)(2,1)S(1)} %copy-done.3, bf16[256,512]{1,0:T(8,128)(2,1)S(1)} %copy-done.2, bf16[512,256]{1,0:T(8,128)(2,1)S(1)} %copy-done.1, bf16[512,256]{1,0:T(8,128)(2,1)S(1)} %copy-done), custom_call_target="tpu_custom_call" | custom-call | tf_op jit(solution)/shard_map/cross/pallas_call | solution.py:294
  27.6 0.0 copy-start.4
  27.7 0.0 copy-start.5
  27.7 0.0 copy-start.6
  27.7 31.4 %all_to_all.11 = bf16[512,2,128]{2,1,0:T(2,128)(2,1)S(1)} all-to-all(bf16[512,2,128]{2,1,0:T(2,128)(2,1)S(1)} %bitcast.9), channel_id=1, replica_groups=mesh['x'=4,'yh'=2,'core'=2,'z'=8,'yl'=4] {'z','yl','x','yh','core'}, dimensions={0} | all-to-all | bytes 524288 | tf_op jit(solution)/shard_map/all_to_all | solution.py:310
  59.1 0.0 copy-done.4
  59.1 0.0 copy-done.5
  59.1 0.0 copy-done.6
  59.1 0.9 %lag.1 = f32[128,128]{1,0:T(8,128)} custom-call(bf16[1024,128]{1,0:T(8,128)(2,1)S(1)} %bitcast.8, f32[8,128]{1,0:T(8,128)S(1)} %copy-done.6, bf16[128,128]{1,0:T(8,128)(2,1)S(1)} %copy-done.5, bf16[128,128]{1,0:T(8,128)(2,1)S(1)} %copy-done.4), custom_call_target="tpu_custom_call" | custom-call | tf_op jit(solution)/shard_map/lag/pallas_call | solution.py:312
Async XLA Ops:
  0.0 26.0 %copy-start.1 = (bf16[512,256]{1,0:T(8,128)(2,1)S(1)}, bf16[512,256]{1,0:T(8,128)(2,1)}, u32[]{:S(2)}) copy-start(bf16[512,256]{1,0:T(8,128)(2,1)} %constant.28.clone.back_high) | copy-start | bytes 786436
  0.0 26.0 %copy-start.2 = (bf16[256,512]{1,0:T(8,128)(2,1)S(1)}, bf16[256,512]{1,0:T(8,128)(2,1)}, u32[]{:S(2)}) copy-start(bf16[256,512]{1,0:T(8,128)(2,1)} %constant.27.clone.to_low) | copy-start | bytes 786436
  0.0 26.0 %copy-start.3 = (bf16[256,512]{1,0:T(8,128)(2,1)S(1)}, bf16[256,512]{1,0:T(8,128)(2,1)}, u32[]{:S(2)}) copy-start(bf16[256,512]{1,0:T(8,128)(2,1)} %constant.26.clone.to_high) | copy-start | bytes 786436
  2.6 23.4 %copy-start = (bf16[512,256]{1,0:T(8,128)(2,1)S(1)}, bf16[512,256]{1,0:T(8,128)(2,1)}, u32[]{:S(2)}) copy-start(bf16[512,256]{1,0:T(8,128)(2,1)} %constant.29.clone.back_low) | copy-start | bytes 786436
  27.6 31.4 %copy-start.4 = (bf16[128,128]{1,0:T(8,128)(2,1)S(1)}, bf16[128,128]{1,0:T(8,128)(2,1)}, u32[]{:S(2)}) copy-start(bf16[128,128]{1,0:T(8,128)(2,1)} %constant.31.clone.table_low) | copy-start | bytes 98308
  27.7 31.4 %copy-start.5 = (bf16[128,128]{1,0:T(8,128)(2,1)S(1)}, bf16[128,128]{1,0:T(8,128)(2,1)}, u32[]{:S(2)}) copy-start(bf16[128,128]{1,0:T(8,128)(2,1)} %constant.30.clone.table_high) | copy-start | bytes 98308
  27.7 31.4 %copy-start.6 = (f32[8,128]{1,0:T(8,128)S(1)}, f32[8,128]{1,0:T(8,128)}, u32[]{:S(2)}) copy-start(f32[8,128]{1,0:T(8,128)} %get-tuple-element.8.weight) | copy-start | bytes 12292

commit v3 on v2

--- a/solution.py
+++ b/solution.py
@@ -17,7 +17,7 @@
 WATER = 0.1
 CHANNELS = 128
 SAMPLES = 512
-PADDED = 256
+PADDED = 192
 WINDOWS = 4
 BLOCKS = 16
 GROUPS = 32
@@ -53,16 +53,27 @@
 
 def channel_table():
     turn = angles(np.arange(CHANNELS), np.arange(PADDED), PADDED)
-    top = np.concatenate([np.cos(turn), -np.sin(turn)], axis=1)
-    bottom = np.concatenate([np.sin(turn), np.cos(turn)], axis=1)
-    return split_table(np.concatenate([top, bottom], axis=0))
+    real_part = np.concatenate([np.cos(turn), np.sin(turn)], axis=0)
+    imag_part = np.concatenate([-np.sin(turn), np.cos(turn)], axis=0)
+    real_rest, imag_rest = real_part[:, 128:], imag_part[:, 128:]
+    return split_table(
+        np.concatenate(
+            [real_part[:, :128], imag_part[:, :128], real_rest, imag_rest, imag_rest, real_rest],
+            axis=1,
+        )
+    )
 
 
 def offset_table():
     turn = angles(np.arange(PADDED), np.arange(OFFSETS) - OFFSETS // 2, PADDED)
-    top = np.concatenate([np.cos(turn), np.sin(turn)], axis=1)
-    bottom = np.concatenate([-np.sin(turn), np.cos(turn)], axis=1)
-    return split_table(np.concatenate([top, bottom], axis=0) / PADDED)
+    of_real = np.concatenate([np.cos(turn), np.sin(turn)], axis=1) / PADDED
+    of_imag = np.concatenate([-np.sin(turn), np.cos(turn)], axis=1) / PADDED
+    real_rest, imag_rest = of_real[128:], of_imag[128:]
+    return split_table(
+        np.concatenate(
+            [of_real[:128], of_imag[:128], real_rest, real_rest, imag_rest, -imag_rest], axis=0
+        )
+    )
 
 
 def lag_table():
@@ -113,7 +124,7 @@
     rows,
     small_sems,
     table_sem,
-    trace_sems,
+    trace_sem,
 ):
     small = [
         pltpu.make_async_copy(source, target, small_sems.at[k])
@@ -122,13 +133,9 @@
         )
     ]
     whole_table = pltpu.make_async_copy(table_hbm, table, table_sem)
-    parts = [
-        pltpu.make_async_copy(traces_hbm.at[window], traces.at[window], trace_sems.at[window])
-        for window in range(WINDOWS)
-    ]
+    whole_traces = pltpu.make_async_copy(traces_hbm, traces, trace_sem)
     whole_table.start()
-    for copy in parts:
-        copy.start()
+    whole_traces.start()
     for copy in small:
         copy.start()
     for copy in small:
@@ -157,8 +164,7 @@
         rows[pl.ds(part * 8 * CHUNK + 8, 8, stride=CHUNK), :] = count_row
         rows[pl.ds(part * 8 * CHUNK + 9, 8, stride=CHUNK), :] = owner_row
     whole_table.wait()
-    for copy in parts:
-        copy.wait()
+    whole_traces.wait()
     flat = traces[...].reshape(WINDOWS * CHANNELS, SAMPLES)
     both = lax.dot_general(
         table[...], flat, (((1,), (1,)), ((), ())), preferred_element_type=F32
@@ -179,7 +185,7 @@
 
 
 def cross_kernel(
-    chunks, to_high, to_low, back_high, back_low, out, rows, stacked, spectra, cross, slots
+    chunks, to_high, to_low, back_high, back_low, out, rows, stacked, spectra, cross, pieces, named
 ):
     rows[...] = chunks[...].astype(F32)
     block_rows = BLOCKS * CHUNK
@@ -212,45 +218,55 @@
             jnp.broadcast_to(counts[group][:, step : step + 1], (BLOCKS, 128))
             for group in range(PLANE_GROUPS)
         ]
+        here = slice(step * BLOCKS, (step + 1) * BLOCKS)
         for half in range(2):
-            total_real = jnp.zeros((BLOCKS, 128), F32)
-            total_imag = jnp.zeros((BLOCKS, 128), F32)
+            first = jnp.zeros((BLOCKS, 128), F32)
+            second = jnp.zeros((BLOCKS, 128), F32)
             for group in range(PLANE_GROUPS):
                 for window in range(WINDOWS):
                     base = (group * WINDOWS + window) * EXTENDED + SPAN
                     own = slice(base, base + BLOCKS)
                     before = slice(base - distance, base - distance + BLOCKS)
-                    own_real = spectra[half, own, :]
-                    own_imag = spectra[2 + half, own, :]
-                    src_real = spectra[half, before, :]
-                    src_imag = spectra[2 + half, before, :]
-                    term_real = src_real * own_real + src_imag * own_imag
-                    term_imag = src_real * own_imag - src_imag * own_real
+                    if half == 0:
+                        own_real = spectra[0, own, :]
+                        own_imag = spectra[1, own, :]
+                        src_real = spectra[0, before, :]
+                        src_imag = spectra[1, before, :]
+                        term_first = src_real * own_real + src_imag * own_imag
+                        term_second = src_real * own_imag - src_imag * own_real
+                    else:
+                        source = spectra[2, before, :]
+                        term_first = source * spectra[2, own, :]
+                        term_second = source * spectra[3, own, :]
                     if window > 0:
                         keep = limits[group] > float(window)
-                        term_real = jnp.where(keep, term_real, 0.0)
-                        term_imag = jnp.where(keep, term_imag, 0.0)
-                    total_real = total_real + term_real
-                    total_imag = total_imag + term_imag
-            here = slice(step * BLOCKS, (step + 1) * BLOCKS)
-            cross[here, half * 128 : (half + 1) * 128] = total_real
-            cross[here, PADDED + half * 128 : PADDED + (half + 1) * 128] = total_imag
-    partial = dot_split(cross[...], back_high[...], back_low[...])
+                        term_first = jnp.where(keep, term_first, 0.0)
+                        term_second = jnp.where(keep, term_second, 0.0)
+                    first = first + term_first
+                    second = second + term_second
+            cross[here, half * 256 : half * 256 + 128] = first
+            cross[here, half * 256 + 128 : half * 256 + 256] = second
+        chosen = jnp.broadcast_to(owners[:, step : step + 1], (BLOCKS, 128))
+        for half in range(2):
+            named[pl.ds(step * 2 * BLOCKS + half, BLOCKS, stride=2), :] = chosen
+    high, low = split(cross[...])
+    pairs = SPAN * BLOCKS
+    by_high = dot(jnp.concatenate([high, low], axis=0), back_high[...])
+    partial = by_high[:pairs] + (by_high[pairs:] + dot(high, back_low[...]))
+    for half in range(2):
+        pieces[pl.ds(half, pairs, stride=2), :] = partial[:, half * 128 : (half + 1) * 128]
+    lines = 2 * BLOCKS
+    piece_of = [
+        pieces[step * lines : (step + 1) * lines, :].astype(BF16) for step in range(SPAN)
+    ]
     owner_of = [
-        jnp.broadcast_to(owners[:, step : step + 1], (BLOCKS, 128)) for step in range(SPAN)
+        named[step * lines : (step + 1) * lines, :].astype(BF16) for step in range(SPAN)
     ]
     for owner in range(GROUPS):
-        halves = [jnp.zeros((BLOCKS, 128), F32), jnp.zeros((BLOCKS, 128), F32)]
+        chunk = jnp.zeros((lines, OFFSETS), BF16)
         for step in range(SPAN):
-            chosen = owner_of[step] == float(owner)
-            for half in range(2):
-                piece = partial[
-                    step * BLOCKS : (step + 1) * BLOCKS, half * 128 : (half + 1) * 128
-                ]
-                halves[half] = jnp.where(chosen, piece, halves[half])
-        for half in range(2):
-            slots[pl.ds(owner * 2 * BLOCKS + half, BLOCKS, stride=2), :] = halves[half]
-    out[...] = slots[...].astype(BF16)
+            chunk = jnp.where(owner_of[step] == jnp.bfloat16(owner), piece_of[step], chunk)
+        out[owner * lines : (owner + 1) * lines, :] = chunk
 
 
 def lag_kernel(arrived, weight, table_high, table_low, out):
@@ -283,11 +299,17 @@
             pltpu.VMEM((BAND * CHUNK, CHANNELS), F32),
             pltpu.SemaphoreType.DMA((3,)),
             pltpu.SemaphoreType.DMA,
-            pltpu.SemaphoreType.DMA((WINDOWS,)),
+            pltpu.SemaphoreType.DMA,
         ],
-        compiler_params=pltpu.CompilerParams(vmem_limit_bytes=60 << 20),
+        compiler_params=pltpu.CompilerParams(vmem_limit_bytes=32 << 20),
         name="whiten",
-    )(place, pair_listed, owner_slot, window_count[0], traces[0], band_table())
+    )(
+        place,
+        *(
+            pltpu.with_memory_space_constraint(operand, pltpu.HBM)
+            for operand in (pair_listed, owner_slot, window_count[0], traces[0], band_table())
+        ),
+    )
     chunks = chunks.reshape(BAND, CHUNK // 2, 2, CHANNELS)
     chunks = lax.all_to_all(chunks, PLANE, 0, 0, tiled=True)
     chunks = chunks.reshape(BAND * CHUNK, CHANNELS)
@@ -300,8 +322,9 @@
             pltpu.VMEM((BAND * CHUNK, CHANNELS), F32),
             pltpu.VMEM((PLANE_GROUPS * WINDOWS * BLOCKS, 2 * CHANNELS), F32),
             pltpu.VMEM((4, PLANE_GROUPS * WINDOWS * EXTENDED, 128), F32),
-            pltpu.VMEM((SPAN * BLOCKS, 2 * PADDED), F32),
-            pltpu.VMEM((GROUPS * BLOCKS * 2, OFFSETS), F32),
+            pltpu.VMEM((SPAN * BLOCKS, 512), F32),
+            pltpu.VMEM((SPAN * BLOCKS * 2, OFFSETS), F32),
+            pltpu.VMEM((SPAN * BLOCKS * 2, OFFSETS), F32),
         ],
         compiler_params=pltpu.CompilerParams(vmem_limit_bytes=32 << 20),
         name="cross",

time: 60.2 us -> 58.8 us (0.977)
  Pallas kernels: 5.13 us -> 3.94 us
    pallas_call x1, Pallas kernels: 2.59 us -> 1.86 us  [shards(): pl.pallas_call(whiten_kernel, out_shape=(jax.ShapeDtypeStruct((BAND * CHU...]
where the time goes in v3:
time: 58.8 us; the launch traced here: 58.6 us
  blocking collectives  54.5 us (93%)
  Pallas kernels  3.94 us (7%)
    all_to_all x1, blocking collectives, shards(): slots = lax.all_to_all(slots, WHOLE, 0, 0, tiled=True)  31.4 us
    all_to_all x1, blocking collectives, shards(): chunks = lax.all_to_all(chunks, PLANE, 0, 0, tiled=True)  23.1 us
    pallas_call x1, Pallas kernels, shards(): pl.pallas_call(whiten_kernel, out_shape=(jax.ShapeDtypeStruct((BAND * CHU...  1.86 us
    pallas_call x1, Pallas kernels, shards(): pl.pallas_call(cross_kernel, out_shape=jax.ShapeDtypeStruct((GROUPS * BLO...  1.21 us

profile of v3, /device:TPU:1, one launch (start us, length us, event | category | flops | bytes accessed | tf_op | source)
XLA Modules:
  0.0 58.6 jit_solution(2828359284322380619)
XLA Ops:
  0.0 0.0 copy-start.1
  0.0 0.0 copy-start.2
  0.0 0.0 copy-start.3
  0.0 1.9 %whiten.1 = (bf16[640,128]{1,0:T(8,128)(2,1)S(1)}, f32[8,128]{1,0:T(8,128)S(1)}) custom-call(s32[1]{0:T(128)} %bitcast.place, s32[1,8]{1,0:T(1,128)} %listed_hbm.1, s32[1,8]{1,0:T(1,128)} %owners_hbm.1, s32[8,32]{1,0:T(8,128)} %bitcast.13, bf16[4,128,512]{2,1,0:T(8,128)(2,1)} %bitcast.12, bf16[256,512]{1,0:T(8,128)(2,1)} %constant.25.clone.table_hbm), custom_call_target="tpu_custom_call" | custom-call | tf_op jit(solution)/shard_map/whiten/pallas_call | solution.py:285
  1.9 0.0 copy-start
  1.9 23.1 %all_to_all.10 = bf16[64,5,2,128]{3,2,1,0:T(2,128)(2,1)S(1)} all-to-all(bf16[64,5,2,128]{3,2,1,0:T(2,128)(2,1)S(1)} %bitcast.11), channel_id=1, replica_groups=mesh['x'=4,'yh'=2,'core'=2,'z'=8,'yl'=4] {'yl','x','yh','core'}, dimensions={0} | all-to-all | bytes 327680 | tf_op jit(solution)/shard_map/all_to_all | solution.py:314
  25.0 0.0 copy-done.1
  25.0 0.0 copy-done.2
  25.0 0.0 copy-done.3
  25.0 0.0 copy-done
  25.0 1.2 %cross.1 = bf16[1024,128]{1,0:T(8,128)(2,1)S(1)} custom-call(bf16[640,128]{1,0:T(8,128)(2,1)S(1)} %bitcast.10, bf16[256,512]{1,0:T(8,128)(2,1)S(1)} %copy-done.3, bf16[256,512]{1,0:T(8,128)(2,1)S(1)} %copy-done.2, bf16[512,256]{1,0:T(8,128)(2,1)S(1)} %copy-done.1, bf16[512,256]{1,0:T(8,128)(2,1)S(1)} %copy-done), custom_call_target="tpu_custom_call" | custom-call | tf_op jit(solution)/shard_map/cross/pallas_call | solution.py:316
  26.3 0.0 copy-start.4
  26.3 0.0 copy-start.5
  26.3 31.4 %all_to_all.11 = bf16[512,2,128]{2,1,0:T(2,128)(2,1)S(1)} all-to-all(bf16[512,2,128]{2,1,0:T(2,128)(2,1)S(1)} %bitcast.9), channel_id=1, replica_groups=mesh['x'=4,'yh'=2,'core'=2,'z'=8,'yl'=4] {'z','yl','x','yh','core'}, dimensions={0} | all-to-all | bytes 524288 | tf_op jit(solution)/shard_map/all_to_all | solution.py:333
  57.7 0.0 copy-done.4
  57.7 0.0 copy-done.5
  57.7 0.9 %lag.1 = f32[128,128]{1,0:T(8,128)} custom-call(bf16[1024,128]{1,0:T(8,128)(2,1)S(1)} %bitcast.8, f32[8,128]{1,0:T(8,128)S(1)} %get-tuple-element.8.weight, bf16[128,128]{1,0:T(8,128)(2,1)S(1)} %copy-done.5, bf16[128,128]{1,0:T(8,128)(2,1)S(1)} %copy-done.4), custom_call_target="tpu_custom_call" | custom-call | tf_op jit(solution)/shard_map/lag/pallas_call | solution.py:335
Async XLA Ops:
  0.0 25.0 %copy-start.1 = (bf16[512,256]{1,0:T(8,128)(2,1)S(1)}, bf16[512,256]{1,0:T(8,128)(2,1)}, u32[]{:S(2)}) copy-start(bf16[512,256]{1,0:T(8,128)(2,1)} %constant.28.clone.back_high) | copy-start | bytes 786436
  0.0 25.0 %copy-start.2 = (bf16[256,512]{1,0:T(8,128)(2,1)S(1)}, bf16[256,512]{1,0:T(8,128)(2,1)}, u32[]{:S(2)}) copy-start(bf16[256,512]{1,0:T(8,128)(2,1)} %constant.27.clone.to_low) | copy-start | bytes 786436
  0.0 25.0 %copy-start.3 = (bf16[256,512]{1,0:T(8,128)(2,1)S(1)}, bf16[256,512]{1,0:T(8,128)(2,1)}, u32[]{:S(2)}) copy-start(bf16[256,512]{1,0:T(8,128)(2,1)} %constant.26.clone.to_high) | copy-start | bytes 786436
  1.9 23.2 %copy-start = (bf16[512,256]{1,0:T(8,128)(2,1)S(1)}, bf16[512,256]{1,0:T(8,128)(2,1)}, u32[]{:S(2)}) copy-start(bf16[512,256]{1,0:T(8,128)(2,1)} %constant.29.clone.back_low) | copy-start | bytes 786436
  26.3 31.4 %copy-start.4 = (bf16[128,128]{1,0:T(8,128)(2,1)S(1)}, bf16[128,128]{1,0:T(8,128)(2,1)}, u32[]{:S(2)}) copy-start(bf16[128,128]{1,0:T(8,128)(2,1)} %constant.31.clone.table_low) | copy-start | bytes 98308
  26.3 31.4 %copy-start.5 = (bf16[128,128]{1,0:T(8,128)(2,1)S(1)}, bf16[128,128]{1,0:T(8,128)(2,1)}, u32[]{:S(2)}) copy-start(bf16[128,128]{1,0:T(8,128)(2,1)} %constant.30.clone.table_high) | copy-start | bytes 98308

commit v4 on v3

--- a/solution.py
+++ b/solution.py
@@ -185,20 +185,24 @@
 
 
 def cross_kernel(
-    chunks, to_high, to_low, back_high, back_low, out, rows, stacked, spectra, cross, pieces, named
+    chunks, to_high, to_low, back_high, back_low, out, rows, spectra, cross, pieces, named
 ):
     rows[...] = chunks[...].astype(F32)
     block_rows = BLOCKS * CHUNK
-    for group in range(PLANE_GROUPS):
-        for window in range(WINDOWS):
-            base = (group * WINDOWS + window) * BLOCKS
-            for part in range(2):
-                start = group * block_rows + part * WINDOWS + window
-                lanes = slice(part * CHANNELS, (part + 1) * CHANNELS)
-                stacked[base : base + BLOCKS, lanes] = rows[
-                    pl.ds(start, BLOCKS, stride=CHUNK), :
-                ]
-    block_data = stacked[...].astype(BF16)
+    block_data = jnp.concatenate(
+        [
+            jnp.concatenate(
+                [
+                    rows[pl.ds(group * block_rows + part * WINDOWS + window, BLOCKS, stride=CHUNK), :]
+                    for part in range(2)
+                ],
+                axis=1,
+            ).astype(BF16)
+            for group in range(PLANE_GROUPS)
+            for window in range(WINDOWS)
+        ],
+        axis=0,
+    )
     both = dot(block_data, to_high[...]) + dot(block_data, to_low[...])
     for tile in range(4):
         lanes = slice(tile * 128, (tile + 1) * 128)
@@ -227,23 +231,23 @@
                     base = (group * WINDOWS + window) * EXTENDED + SPAN
                     own = slice(base, base + BLOCKS)
                     before = slice(base - distance, base - distance + BLOCKS)
+                    keep = limits[group] > float(window)
                     if half == 0:
                         own_real = spectra[0, own, :]
                         own_imag = spectra[1, own, :]
                         src_real = spectra[0, before, :]
                         src_imag = spectra[1, before, :]
-                        term_first = src_real * own_real + src_imag * own_imag
-                        term_second = src_real * own_imag - src_imag * own_real
+                        if window > 0:
+                            src_real = jnp.where(keep, src_real, 0.0)
+                            src_imag = jnp.where(keep, src_imag, 0.0)
+                        first = first + (src_real * own_real + src_imag * own_imag)
+                        second = second + (src_real * own_imag - src_imag * own_real)
                     else:
                         source = spectra[2, before, :]
-                        term_first = source * spectra[2, own, :]
-                        term_second = source * spectra[3, own, :]
-                    if window > 0:
-                        keep = limits[group] > float(window)
-                        term_first = jnp.where(keep, term_first, 0.0)
-                        term_second = jnp.where(keep, term_second, 0.0)
-                    first = first + term_first
-                    second = second + term_second
+                        if window > 0:
+                            source = jnp.where(keep, source, 0.0)
+                        first = first + source * spectra[2, own, :]
+                        second = second + source * spectra[3, own, :]
             cross[here, half * 256 : half * 256 + 128] = first
             cross[here, half * 256 + 128 : half * 256 + 256] = second
         chosen = jnp.broadcast_to(owners[:, step : step + 1], (BLOCKS, 128))
@@ -320,7 +324,6 @@
         out_specs=vmem,
         scratch_shapes=[
             pltpu.VMEM((BAND * CHUNK, CHANNELS), F32),
-            pltpu.VMEM((PLANE_GROUPS * WINDOWS * BLOCKS, 2 * CHANNELS), F32),
             pltpu.VMEM((4, PLANE_GROUPS * WINDOWS * EXTENDED, 128), F32),
             pltpu.VMEM((SPAN * BLOCKS, 512), F32),
             pltpu.VMEM((SPAN * BLOCKS * 2, OFFSETS), F32),

time: 58.8 us -> 58.7 us (level)
  no operation moved by 1% of the time
where the time goes in v4:
time: 58.7 us; the launch traced here: 58.5 us
  blocking collectives  54.5 us (93%)
  Pallas kernels  3.89 us (7%)
    all_to_all x1, blocking collectives, shards(): slots = lax.all_to_all(slots, WHOLE, 0, 0, tiled=True)  31.4 us
    all_to_all x1, blocking collectives, shards(): chunks = lax.all_to_all(chunks, PLANE, 0, 0, tiled=True)  23.1 us
    pallas_call x1, Pallas kernels, shards(): pl.pallas_call(whiten_kernel, out_shape=(jax.ShapeDtypeStruct((BAND * CHU...  1.86 us

profile of v4, /device:TPU:1, one launch (start us, length us, event | category | flops | bytes accessed | tf_op | source)
XLA Modules:
  0.0 58.5 jit_solution(5637343247771964879)
XLA Ops:
  0.0 0.0 copy-start.1
  0.0 0.0 copy-start.2
  0.0 0.0 copy-start.3
  0.0 1.9 %whiten.1 = (bf16[640,128]{1,0:T(8,128)(2,1)S(1)}, f32[8,128]{1,0:T(8,128)S(1)}) custom-call(s32[1]{0:T(128)} %bitcast.place, s32[1,8]{1,0:T(1,128)} %listed_hbm.1, s32[1,8]{1,0:T(1,128)} %owners_hbm.1, s32[8,32]{1,0:T(8,128)} %bitcast.13, bf16[4,128,512]{2,1,0:T(8,128)(2,1)} %bitcast.12, bf16[256,512]{1,0:T(8,128)(2,1)} %constant.25.clone.table_hbm), custom_call_target="tpu_custom_call" | custom-call | tf_op jit(solution)/shard_map/whiten/pallas_call | solution.py:289
  1.9 0.0 copy-start
  1.9 23.1 %all_to_all.10 = bf16[64,5,2,128]{3,2,1,0:T(2,128)(2,1)S(1)} all-to-all(bf16[64,5,2,128]{3,2,1,0:T(2,128)(2,1)S(1)} %bitcast.11), channel_id=1, replica_groups=mesh['x'=4,'yh'=2,'core'=2,'z'=8,'yl'=4] {'yl','x','yh','core'}, dimensions={0} | all-to-all | bytes 327680 | tf_op jit(solution)/shard_map/all_to_all | solution.py:318
  25.0 0.0 copy-done.1
  25.0 0.0 copy-done.2
  25.0 0.0 copy-done.3
  25.0 0.0 copy-done
  25.0 1.2 %cross.1 = bf16[1024,128]{1,0:T(8,128)(2,1)S(1)} custom-call(bf16[640,128]{1,0:T(8,128)(2,1)S(1)} %bitcast.10, bf16[256,512]{1,0:T(8,128)(2,1)S(1)} %copy-done.3, bf16[256,512]{1,0:T(8,128)(2,1)S(1)} %copy-done.2, bf16[512,256]{1,0:T(8,128)(2,1)S(1)} %copy-done.1, bf16[512,256]{1,0:T(8,128)(2,1)S(1)} %copy-done), custom_call_target="tpu_custom_call" | custom-call | tf_op jit(solution)/shard_map/cross/pallas_call | solution.py:320
  26.2 0.0 copy-start.4
  26.2 0.0 copy-start.5
  26.2 31.4 %all_to_all.11 = bf16[512,2,128]{2,1,0:T(2,128)(2,1)S(1)} all-to-all(bf16[512,2,128]{2,1,0:T(2,128)(2,1)S(1)} %bitcast.9), channel_id=1, replica_groups=mesh['x'=4,'yh'=2,'core'=2,'z'=8,'yl'=4] {'z','yl','x','yh','core'}, dimensions={0} | all-to-all | bytes 524288 | tf_op jit(solution)/shard_map/all_to_all | solution.py:336
  57.6 0.0 copy-done.4
  57.6 0.0 copy-done.5
  57.6 0.9 %lag.1 = f32[128,128]{1,0:T(8,128)} custom-call(bf16[1024,128]{1,0:T(8,128)(2,1)S(1)} %bitcast.8, f32[8,128]{1,0:T(8,128)S(1)} %get-tuple-element.8.weight, bf16[128,128]{1,0:T(8,128)(2,1)S(1)} %copy-done.5, bf16[128,128]{1,0:T(8,128)(2,1)S(1)} %copy-done.4), custom_call_target="tpu_custom_call" | custom-call | tf_op jit(solution)/shard_map/lag/pallas_call | solution.py:338
Async XLA Ops:
  0.0 25.0 %copy-start.1 = (bf16[512,256]{1,0:T(8,128)(2,1)S(1)}, bf16[512,256]{1,0:T(8,128)(2,1)}, u32[]{:S(2)}) copy-start(bf16[512,256]{1,0:T(8,128)(2,1)} %constant.28.clone.back_high) | copy-start | bytes 786436
  0.0 25.0 %copy-start.2 = (bf16[256,512]{1,0:T(8,128)(2,1)S(1)}, bf16[256,512]{1,0:T(8,128)(2,1)}, u32[]{:S(2)}) copy-start(bf16[256,512]{1,0:T(8,128)(2,1)} %constant.27.clone.to_low) | copy-start | bytes 786436
  0.0 25.0 %copy-start.3 = (bf16[256,512]{1,0:T(8,128)(2,1)S(1)}, bf16[256,512]{1,0:T(8,128)(2,1)}, u32[]{:S(2)}) copy-start(bf16[256,512]{1,0:T(8,128)(2,1)} %constant.26.clone.to_high) | copy-start | bytes 786436
  1.9 23.2 %copy-start = (bf16[512,256]{1,0:T(8,128)(2,1)S(1)}, bf16[512,256]{1,0:T(8,128)(2,1)}, u32[]{:S(2)}) copy-start(bf16[512,256]{1,0:T(8,128)(2,1)} %constant.29.clone.back_low) | copy-start | bytes 786436
  26.2 31.4 %copy-start.4 = (bf16[128,128]{1,0:T(8,128)(2,1)S(1)}, bf16[128,128]{1,0:T(8,128)(2,1)}, u32[]{:S(2)}) copy-start(bf16[128,128]{1,0:T(8,128)(2,1)} %constant.31.clone.table_low) | copy-start | bytes 98308
  26.2 31.4 %copy-start.5 = (bf16[128,128]{1,0:T(8,128)(2,1)S(1)}, bf16[128,128]{1,0:T(8,128)(2,1)}, u32[]{:S(2)}) copy-start(bf16[128,128]{1,0:T(8,128)(2,1)} %constant.30.clone.table_high) | copy-start | bytes 98308

commit v5 on v4

--- a/solution.py
+++ b/solution.py
@@ -29,7 +29,8 @@
 CHAN = ("x", "yh", "core")
 TM = ("z", "yl")
 PLANE = ("yl",) + CHAN
-WHOLE = TM + CHAN
+WHOLE = ("yl", "z", "core", "yh", "x")
+DEPTH = GROUPS // PLANE_GROUPS
 F32 = jnp.float32
 BF16 = jnp.bfloat16
 
@@ -76,8 +77,20 @@
     )
 
 
+def block_order():
+    return np.arange(BLOCKS).reshape(4, 2, 2).transpose(2, 1, 0).reshape(-1)
+
+
+def order_table():
+    pairs = SPAN * BLOCKS
+    step, block, half = np.meshgrid(np.arange(SPAN), block_order(), np.arange(2), indexing="ij")
+    source = (half * pairs + step * BLOCKS + block).reshape(-1)
+    return (source[:, None] == np.arange(2 * pairs)[None, :]).astype(ml_dtypes.bfloat16)
+
+
 def lag_table():
-    turn = angles(np.arange(BAND) + 1, np.arange(LAGS) - LAGS // 2, SAMPLES)
+    bins = (np.arange(PLANE_GROUPS)[:, None] * BLOCKS + block_order()[None, :]).reshape(-1) + 1
+    turn = angles(bins, np.arange(LAGS) - LAGS // 2, SAMPLES)
     pair = np.stack([np.cos(turn), -np.sin(turn)], axis=1).reshape(2 * BAND, LAGS)
     return split_table(pair / math.sqrt(BAND))
 
@@ -185,7 +198,7 @@
 
 
 def cross_kernel(
-    chunks, to_high, to_low, back_high, back_low, out, rows, spectra, cross, pieces, named
+    chunks, to_high, to_low, back_high, back_low, order, out, rows, spectra, cross
 ):
     rows[...] = chunks[...].astype(F32)
     block_rows = BLOCKS * CHUNK
@@ -250,33 +263,47 @@
                         second = second + source * spectra[3, own, :]
             cross[here, half * 256 : half * 256 + 128] = first
             cross[here, half * 256 + 128 : half * 256 + 256] = second
-        chosen = jnp.broadcast_to(owners[:, step : step + 1], (BLOCKS, 128))
-        for half in range(2):
-            named[pl.ds(step * 2 * BLOCKS + half, BLOCKS, stride=2), :] = chosen
     high, low = split(cross[...])
     pairs = SPAN * BLOCKS
     by_high = dot(jnp.concatenate([high, low], axis=0), back_high[...])
     partial = by_high[:pairs] + (by_high[pairs:] + dot(high, back_low[...]))
-    for half in range(2):
-        pieces[pl.ds(half, pairs, stride=2), :] = partial[:, half * 128 : (half + 1) * 128]
+    named = jnp.concatenate(
+        [
+            jnp.broadcast_to(owners[:, step : step + 1], (BLOCKS, OFFSETS))
+            for step in range(SPAN)
+        ],
+        axis=0,
+    )
+    beside = jnp.concatenate(
+        [
+            jnp.concatenate([partial[:, :OFFSETS], named], axis=1),
+            jnp.concatenate([partial[:, OFFSETS:], named], axis=1),
+        ],
+        axis=0,
+    )
+    ordered = dot(order[...], beside.astype(BF16)).astype(BF16)
     lines = 2 * BLOCKS
-    piece_of = [
-        pieces[step * lines : (step + 1) * lines, :].astype(BF16) for step in range(SPAN)
-    ]
-    owner_of = [
-        named[step * lines : (step + 1) * lines, :].astype(BF16) for step in range(SPAN)
-    ]
-    for owner in range(GROUPS):
+    for slot in range(GROUPS):
+        owner = slot % DEPTH * PLANE_GROUPS + slot // DEPTH
         chunk = jnp.zeros((lines, OFFSETS), BF16)
         for step in range(SPAN):
-            chunk = jnp.where(owner_of[step] == jnp.bfloat16(owner), piece_of[step], chunk)
-        out[owner * lines : (owner + 1) * lines, :] = chunk
+            here = slice(step * lines, (step + 1) * lines)
+            chosen = ordered[here, OFFSETS:] == jnp.bfloat16(owner)
+            chunk = jnp.where(chosen, ordered[here, :OFFSETS], chunk)
+        out[slot * lines : (slot + 1) * lines, :] = chunk
 
 
 def lag_kernel(arrived, weight, table_high, table_low, out):
-    summed = arrived[: 2 * BAND].astype(F32)
-    for layer in range(1, 8):
-        summed = summed + arrived[layer * 2 * BAND : (layer + 1) * 2 * BAND].astype(F32)
+    lines = 2 * BLOCKS
+    sums = []
+    for group in range(PLANE_GROUPS):
+        first = group * DEPTH * lines
+        total = arrived[first : first + lines].astype(F32)
+        for layer in range(1, DEPTH):
+            start = first + layer * lines
+            total = total + arrived[start : start + lines].astype(F32)
+        sums.append(total)
+    summed = jnp.concatenate(sums, axis=0)
     lagged = dot_split(summed.T, table_high[...], table_low[...])
     out[...] = lagged * weight[:1]
 
@@ -320,18 +347,16 @@
     slots = pl.pallas_call(
         cross_kernel,
         out_shape=jax.ShapeDtypeStruct((GROUPS * BLOCKS * 2, OFFSETS), BF16),
-        in_specs=[vmem] * 5,
+        in_specs=[vmem] * 6,
         out_specs=vmem,
         scratch_shapes=[
             pltpu.VMEM((BAND * CHUNK, CHANNELS), F32),
             pltpu.VMEM((4, PLANE_GROUPS * WINDOWS * EXTENDED, 128), F32),
             pltpu.VMEM((SPAN * BLOCKS, 512), F32),
-            pltpu.VMEM((SPAN * BLOCKS * 2, OFFSETS), F32),
-            pltpu.VMEM((SPAN * BLOCKS * 2, OFFSETS), F32),
         ],
         compiler_params=pltpu.CompilerParams(vmem_limit_bytes=32 << 20),
         name="cross",
-    )(chunks, *channel_table(), *offset_table())
+    )(chunks, *channel_table(), *offset_table(), order_table())
     slots = slots.reshape(GROUPS * BLOCKS, 2, OFFSETS)
     slots = lax.all_to_all(slots, WHOLE, 0, 0, tiled=True)
     slots = slots.reshape(GROUPS * BLOCKS * 2, OFFSETS)

time: 58.7 us -> 59.6 us (1.015)
  local copies, waits for them, and re-layouts: 0.03 us -> 0.93 us
    unnamed x12 -> x14, local copies, waits for them, and re-layouts: 0.03 us -> 0.93 us
where the time goes in v5:
time: 59.6 us; the launch traced here: 59.3 us
  blocking collectives  54.3 us (91%)
  Pallas kernels  4.05 us (7%)
  local copies, waits for them, and re-layouts  0.93 us (2%)
    all_to_all x1, blocking collectives, shards(): slots = lax.all_to_all(slots, WHOLE, 0, 0, tiled=True)  31.2 us
    all_to_all x1, blocking collectives, shards(): chunks = lax.all_to_all(chunks, PLANE, 0, 0, tiled=True)  23.1 us
    pallas_call x1, Pallas kernels, shards(): pl.pallas_call(whiten_kernel, out_shape=(jax.ShapeDtypeStruct((BAND * CHU...  1.86 us
    pallas_call x1, Pallas kernels, shards(): pl.pallas_call(cross_kernel, out_shape=jax.ShapeDtypeStruct((GROUPS * BLO...  1.31 us

profile of v5, /device:TPU:1, one launch (start us, length us, event | category | flops | bytes accessed | tf_op | source)
XLA Modules:
  0.0 59.3 jit_solution(16815733840939228597)
XLA Ops:
  0.0 0.0 copy-start.1
  0.0 0.0 copy-start.2
  0.0 0.0 copy-start.3
  0.0 1.9 %whiten.1 = (bf16[640,128]{1,0:T(8,128)(2,1)S(1)}, f32[8,128]{1,0:T(8,128)S(1)}) custom-call(s32[1]{0:T(128)} %bitcast.place, s32[1,8]{1,0:T(1,128)} %listed_hbm.1, s32[1,8]{1,0:T(1,128)} %owners_hbm.1, s32[8,32]{1,0:T(8,128)} %bitcast.13, bf16[4,128,512]{2,1,0:T(8,128)(2,1)} %bitcast.12, bf16[256,512]{1,0:T(8,128)(2,1)} %constant.27.clone.table_hbm), custom_call_target="tpu_custom_call" | custom-call | tf_op jit(solution)/shard_map/whiten/pallas_call | solution.py:316
  1.9 0.0 copy-start
  1.9 23.1 %all_to_all.10 = bf16[64,5,2,128]{3,2,1,0:T(2,128)(2,1)S(1)} all-to-all(bf16[64,5,2,128]{3,2,1,0:T(2,128)(2,1)S(1)} %bitcast.11), channel_id=1, replica_groups=mesh['x'=4,'yh'=2,'core'=2,'z'=8,'yl'=4] {'yl','x','yh','core'}, dimensions={0} | all-to-all | bytes 327680 | tf_op jit(solution)/shard_map/all_to_all | solution.py:345
  25.0 0.0 copy-done.1
  25.0 0.0 copy-done.2
  25.0 0.0 copy-done.3
  25.0 0.0 copy-done
  25.0 0.0 copy-start.4
  25.1 0.9 %copy-done.4 = bf16[256,256]{1,0:T(8,128)(2,1)S(1)} copy-done((bf16[256,256]{1,0:T(8,128)(2,1)S(1)}, bf16[256,256]{1,0:T(8,128)(2,1)}, u32[]{:S(2)}) %copy-start.4) | copy-done | bytes 131096
  25.9 1.3 %cross.1 = bf16[1024,128]{1,0:T(8,128)(2,1)S(1)} custom-call(bf16[640,128]{1,0:T(8,128)(2,1)S(1)} %bitcast.10, bf16[256,512]{1,0:T(8,128)(2,1)S(1)} %copy-done.3, bf16[256,512]{1,0:T(8,128)(2,1)S(1)} %copy-done.2, bf16[512,256]{1,0:T(8,128)(2,1)S(1)} %copy-done.1, bf16[512,256]{1,0:T(8,128)(2,1)S(1)} %copy-done, bf16[256,256]{1,0:T(8,128)(2,1)S(1)} %copy-done.4), custom_call_target="tpu_custom_call" | custom-call | tf_op jit(solution)/shard_map/cross/pallas_call | solution.py:347
  27.3 0.0 copy-start.5
  27.3 0.0 copy-start.6
  27.3 31.2 %all_to_all.11 = bf16[512,2,128]{2,1,0:T(2,128)(2,1)S(1)} all-to-all(bf16[512,2,128]{2,1,0:T(2,128)(2,1)S(1)} %bitcast.8), channel_id=1, replica_groups=mesh['x'=4,'yh'=2,'core'=2,'z'=8,'yl'=4] {'yl','z','core','yh','x'}, dimensions={0} | all-to-all | bytes 524288 | tf_op jit(solution)/shard_map/all_to_all | solution.py:361
  58.4 0.0 copy-done.5
  58.5 0.0 copy-done.6
  58.5 0.9 %lag.1 = f32[128,128]{1,0:T(8,128)} custom-call(bf16[1024,128]{1,0:T(8,128)(2,1)S(1)} %bitcast.9, f32[8,128]{1,0:T(8,128)S(1)} %get-tuple-element.8.weight, bf16[128,128]{1,0:T(8,128)(2,1)S(1)} %copy-done.6, bf16[128,128]{1,0:T(8,128)(2,1)S(1)} %copy-done.5), custom_call_target="tpu_custom_call" | custom-call | tf_op jit(solution)/shard_map/lag/pallas_call | solution.py:363
Async XLA Ops:
  0.0 25.0 %copy-start.1 = (bf16[512,256]{1,0:T(8,128)(2,1)S(1)}, bf16[512,256]{1,0:T(8,128)(2,1)}, u32[]{:S(2)}) copy-start(bf16[512,256]{1,0:T(8,128)(2,1)} %constant.30.clone.back_high) | copy-start | bytes 786436
  0.0 25.0 %copy-start.2 = (bf16[256,512]{1,0:T(8,128)(2,1)S(1)}, bf16[256,512]{1,0:T(8,128)(2,1)}, u32[]{:S(2)}) copy-start(bf16[256,512]{1,0:T(8,128)(2,1)} %constant.29.clone.to_low) | copy-start | bytes 786436
  0.0 25.0 %copy-start.3 = (bf16[256,512]{1,0:T(8,128)(2,1)S(1)}, bf16[256,512]{1,0:T(8,128)(2,1)}, u32[]{:S(2)}) copy-start(bf16[256,512]{1,0:T(8,128)(2,1)} %constant.28.clone.to_high) | copy-start | bytes 786436
  1.9 23.2 %copy-start = (bf16[512,256]{1,0:T(8,128)(2,1)S(1)}, bf16[512,256]{1,0:T(8,128)(2,1)}, u32[]{:S(2)}) copy-start(bf16[512,256]{1,0:T(8,128)(2,1)} %constant.31.clone.back_low) | copy-start | bytes 786436
  25.0 0.9 %copy-start.4 = (bf16[256,256]{1,0:T(8,128)(2,1)S(1)}, bf16[256,256]{1,0:T(8,128)(2,1)}, u32[]{:S(2)}) copy-start(bf16[256,256]{1,0:T(8,128)(2,1)} %constant.32.clone.order) | copy-start | bytes 393220
  27.3 31.2 %copy-start.5 = (bf16[128,128]{1,0:T(8,128)(2,1)S(1)}, bf16[128,128]{1,0:T(8,128)(2,1)}, u32[]{:S(2)}) copy-start(bf16[128,128]{1,0:T(8,128)(2,1)} %constant.34.clone.table_low) | copy-start | bytes 98308
  27.3 31.2 %copy-start.6 = (bf16[128,128]{1,0:T(8,128)(2,1)S(1)}, bf16[128,128]{1,0:T(8,128)(2,1)}, u32[]{:S(2)}) copy-start(bf16[128,128]{1,0:T(8,128)(2,1)} %constant.33.clone.table_high) | copy-start | bytes 98308

commit v6 on v4

--- a/solution.py
+++ b/solution.py
@@ -96,15 +96,13 @@
     return dot(high, table_high) + (dot(low, table_high) + dot(high, table_low))
 
 
-def smooth_sums(amplitude):
-    target = lax.broadcasted_iota(jnp.int32, (2 * BAND, BAND), 0)
-    source = lax.broadcasted_iota(jnp.int32, (2 * BAND, BAND), 1)
+def smooth_matrix():
+    target = lax.broadcasted_iota(jnp.int32, (2 * BAND, 2 * BAND), 0)
+    source = lax.broadcasted_iota(jnp.int32, (2 * BAND, 2 * BAND), 1)
+    source = jnp.where(source >= BAND, source - BAND, source)
     start = jnp.clip(target - SMOOTH // 2, 0, BAND - SMOOTH)
     inside = (target >= BAND) | ((source >= start) & (source < start + SMOOTH))
-    smooth = inside.astype(F32).astype(BF16)
-    high, low = split(amplitude)
-    sums = dot(smooth, high) + dot(smooth, low)
-    return sums[:BAND], sums[BAND:]
+    return inside.astype(F32).astype(BF16)
 
 
 def whiten_kernel(
@@ -122,6 +120,7 @@
     traces,
     table,
     rows,
+    smooth,
     small_sems,
     table_sem,
     trace_sem,
@@ -163,6 +162,7 @@
     for part in range(BAND // 8):
         rows[pl.ds(part * 8 * CHUNK + 8, 8, stride=CHUNK), :] = count_row
         rows[pl.ds(part * 8 * CHUNK + 9, 8, stride=CHUNK), :] = owner_row
+    smooth[...] = smooth_matrix()
     whole_table.wait()
     whole_traces.wait()
     flat = traces[...].reshape(WINDOWS * CHANNELS, SAMPLES)
@@ -173,8 +173,8 @@
     real_part = spectrum[:BAND]
     imag_part = spectrum[BAND:]
     amplitude = jnp.sqrt(real_part * real_part + imag_part * imag_part)
-    near, everywhere = smooth_sums(amplitude)
-    water_level = near / SMOOTH + WATER * (everywhere / BAND) + 1e-6
+    sums = dot(smooth[...], jnp.concatenate(split(amplitude), axis=0))
+    water_level = sums[:BAND] / SMOOTH + WATER * (sums[BAND:] / BAND) + 1e-6
     real_part = real_part / water_level
     imag_part = imag_part / water_level
     for window in range(WINDOWS):
@@ -301,6 +301,7 @@
             pltpu.VMEM((WINDOWS, CHANNELS, SAMPLES), BF16),
             pltpu.VMEM((4 * BAND, SAMPLES), BF16),
             pltpu.VMEM((BAND * CHUNK, CHANNELS), F32),
+            pltpu.VMEM((2 * BAND, 2 * BAND), BF16),
             pltpu.SemaphoreType.DMA((3,)),
             pltpu.SemaphoreType.DMA,
             pltpu.SemaphoreType.DMA,

time: 58.7 us -> 58.7 us (level)
  no operation moved by 1% of the time
where the time goes in v6:
time: 58.7 us; the launch traced here: 58.5 us
  blocking collectives  54.5 us (93%)
  Pallas kernels  3.85 us (7%)
    all_to_all x1, blocking collectives, shards(): slots = lax.all_to_all(slots, WHOLE, 0, 0, tiled=True)  31.4 us
    all_to_all x1, blocking collectives, shards(): chunks = lax.all_to_all(chunks, PLANE, 0, 0, tiled=True)  23.1 us
    pallas_call x1, Pallas kernels, shards(): pl.pallas_call(whiten_kernel, out_shape=(jax.ShapeDtypeStruct((BAND * CHU...  1.82 us

profile of v6, /device:TPU:1, one launch (start us, length us, event | category | flops | bytes accessed | tf_op | source)
XLA Modules:
  0.0 58.5 jit_solution(1413384048996812722)
XLA Ops:
  0.0 0.0 copy-start.1
  0.0 0.0 copy-start.2
  0.0 0.0 copy-start.3
  0.0 1.8 %whiten.1 = (bf16[640,128]{1,0:T(8,128)(2,1)S(1)}, f32[8,128]{1,0:T(8,128)S(1)}) custom-call(s32[1]{0:T(128)} %bitcast.place, s32[1,8]{1,0:T(1,128)} %listed_hbm.1, s32[1,8]{1,0:T(1,128)} %owners_hbm.1, s32[8,32]{1,0:T(8,128)} %bitcast.13, bf16[4,128,512]{2,1,0:T(8,128)(2,1)} %bitcast.12, bf16[256,512]{1,0:T(8,128)(2,1)} %constant.25.clone.table_hbm), custom_call_target="tpu_custom_call" | custom-call | tf_op jit(solution)/shard_map/whiten/pallas_call | solution.py:289
  1.8 0.0 copy-start
  1.9 23.1 %all_to_all.10 = bf16[64,5,2,128]{3,2,1,0:T(2,128)(2,1)S(1)} all-to-all(bf16[64,5,2,128]{3,2,1,0:T(2,128)(2,1)S(1)} %bitcast.11), channel_id=1, replica_groups=mesh['x'=4,'yh'=2,'core'=2,'z'=8,'yl'=4] {'yl','x','yh','core'}, dimensions={0} | all-to-all | bytes 327680 | tf_op jit(solution)/shard_map/all_to_all | solution.py:319
  25.0 0.0 copy-done.1
  25.0 0.0 copy-done.2
  25.0 0.0 copy-done.3
  25.0 0.0 copy-done
  25.0 1.2 %cross.1 = bf16[1024,128]{1,0:T(8,128)(2,1)S(1)} custom-call(bf16[640,128]{1,0:T(8,128)(2,1)S(1)} %bitcast.10, bf16[256,512]{1,0:T(8,128)(2,1)S(1)} %copy-done.3, bf16[256,512]{1,0:T(8,128)(2,1)S(1)} %copy-done.2, bf16[512,256]{1,0:T(8,128)(2,1)S(1)} %copy-done.1, bf16[512,256]{1,0:T(8,128)(2,1)S(1)} %copy-done), custom_call_target="tpu_custom_call" | custom-call | tf_op jit(solution)/shard_map/cross/pallas_call | solution.py:321
  26.2 0.0 copy-start.4
  26.2 0.0 copy-start.5
  26.2 31.4 %all_to_all.11 = bf16[512,2,128]{2,1,0:T(2,128)(2,1)S(1)} all-to-all(bf16[512,2,128]{2,1,0:T(2,128)(2,1)S(1)} %bitcast.9), channel_id=1, replica_groups=mesh['x'=4,'yh'=2,'core'=2,'z'=8,'yl'=4] {'z','yl','x','yh','core'}, dimensions={0} | all-to-all | bytes 524288 | tf_op jit(solution)/shard_map/all_to_all | solution.py:337
  57.6 0.0 copy-done.4
  57.6 0.0 copy-done.5
  57.6 0.9 %lag.1 = f32[128,128]{1,0:T(8,128)} custom-call(bf16[1024,128]{1,0:T(8,128)(2,1)S(1)} %bitcast.8, f32[8,128]{1,0:T(8,128)S(1)} %get-tuple-element.8.weight, bf16[128,128]{1,0:T(8,128)(2,1)S(1)} %copy-done.5, bf16[128,128]{1,0:T(8,128)(2,1)S(1)} %copy-done.4), custom_call_target="tpu_custom_call" | custom-call | tf_op jit(solution)/shard_map/lag/pallas_call | solution.py:339
Async XLA Ops:
  0.0 25.0 %copy-start.1 = (bf16[512,256]{1,0:T(8,128)(2,1)S(1)}, bf16[512,256]{1,0:T(8,128)(2,1)}, u32[]{:S(2)}) copy-start(bf16[512,256]{1,0:T(8,128)(2,1)} %constant.28.clone.back_high) | copy-start | bytes 786436
  0.0 25.0 %copy-start.2 = (bf16[256,512]{1,0:T(8,128)(2,1)S(1)}, bf16[256,512]{1,0:T(8,128)(2,1)}, u32[]{:S(2)}) copy-start(bf16[256,512]{1,0:T(8,128)(2,1)} %constant.27.clone.to_low) | copy-start | bytes 786436
  0.0 25.0 %copy-start.3 = (bf16[256,512]{1,0:T(8,128)(2,1)S(1)}, bf16[256,512]{1,0:T(8,128)(2,1)}, u32[]{:S(2)}) copy-start(bf16[256,512]{1,0:T(8,128)(2,1)} %constant.26.clone.to_high) | copy-start | bytes 786436
  1.8 23.2 %copy-start = (bf16[512,256]{1,0:T(8,128)(2,1)S(1)}, bf16[512,256]{1,0:T(8,128)(2,1)}, u32[]{:S(2)}) copy-start(bf16[512,256]{1,0:T(8,128)(2,1)} %constant.29.clone.back_low) | copy-start | bytes 786436
  26.2 31.4 %copy-start.4 = (bf16[128,128]{1,0:T(8,128)(2,1)S(1)}, bf16[128,128]{1,0:T(8,128)(2,1)}, u32[]{:S(2)}) copy-start(bf16[128,128]{1,0:T(8,128)(2,1)} %constant.31.clone.table_low) | copy-start | bytes 98308
  26.2 31.4 %copy-start.5 = (bf16[128,128]{1,0:T(8,128)(2,1)S(1)}, bf16[128,128]{1,0:T(8,128)(2,1)}, u32[]{:S(2)}) copy-start(bf16[128,128]{1,0:T(8,128)(2,1)} %constant.30.clone.table_high) | copy-start | bytes 98308
